TPU v7x, 512 devices: a whole 4x8x8 slice. The times are simulated.
512 devices in a mesh: dp: 16 (over y, core), item: 32 (over x, z).
Axes of the slice: x: 4, y: 8, z: 8, core: 2. Of those that a mesh axis runs over, the one named last changes fastest.
Arguments:
- query: bfloat16 [512, 256], P(('dp', 'item')), may hold values from -40 to 40
- item_table: bfloat16 [1048576, 256], P(('dp', 'item')), may hold values from -2.5 to 2.5
- context_features: bfloat16 [512, 512], P(('dp', 'item')), may hold values from -6 to 6
- candidates: int32 [512, 1024], P(('dp', 'item')), may hold values from 0 to 1048575, as said below
- lengths: int32 [512], P(('dp', 'item')), may hold values from 128 to 1024, as said below
- logged_slot: int32 [512], P(('dp', 'item')), may hold values from 0 to 1023, as said below
- logging_prop: int32 [512], P(('dp', 'item')), may hold values from 256 to 4095
- w_first: bfloat16 [768, 512], replicated, may hold values from -0.21875 to 0.21875
- w_second: bfloat16 [512, 512], replicated, may hold values from -0.25 to 0.25
- w_score: bfloat16 [512], replicated, may hold values from -0.5 to 0.5
Outputs:
- section_logp: float32 [512, 1024], P(('dp', 'item'))
- log_weight: float32 [512], P(('dp', 'item'))
Inputs may be any that keep to these rules, and one draw needn't show every extreme that they name: `candidates`: item ids. Among the 1024 candidate slots held by one device (its single context), at most 3 name items of any one block of 2048 consecutive ids, and for every device some block is named exactly 3 times. `lengths`: some context's list has 1024 live slots and some context's list has 128. `logged_slot`: below the context's length; the context with the longest list logs its last slot.
All inputs are finite; a program needn't handle non-finite values.
Results may differ from a plain program's by a relative error of at most 0.0003.
Values may be sent and summed in bfloat16 or wider, within the bound.
No kernel may reach another device: no remote copies, remote signals or barrier semaphores. Data moves between devices by JAX's collectives and lax.ppermute only.
A program may use at most 64 MiB of HBM per device.

v0:
```python
import math

import jax
import jax.numpy as jnp
from jax import lax
from jax.sharding import Mesh
from jax.sharding import PartitionSpec as P

DP = ("dp_0", "dp_1")
ITEM = ("item_0", "item_1")
DP_ITEM = ("dp_0", "dp_1", "item_0", "item_1")
ITEM_DP = ("item_0", "item_1", "dp_0", "dp_1")


def in_order(pieces, dim):
    pieces = jnp.moveaxis(pieces, 0, dim)
    shape = pieces.shape
    return pieces.reshape(*shape[:dim], shape[dim] * shape[dim + 1], *shape[dim + 2 :])


def stacked_from(array, axes, order):
    pieces = array[None]
    for k in order:
        pieces = lax.all_gather(pieces, axes[k], axis=0, tiled=True)
    held = [lax.axis_size(axes[k]) for k in reversed(order)]
    pieces = pieces.reshape(*held, *array.shape)
    turned = sorted(range(len(order)), key=lambda place: order[len(order) - 1 - place])
    return pieces.transpose(*turned, *range(len(order), pieces.ndim)).reshape(-1, *array.shape)


def gathered_by_axis(array, axes, order, dim):
    return in_order(stacked_from(array, axes, order), dim)


def all_in_one(array, axis):
    leaves = jax.tree.leaves(array)
    order = sorted(range(len(leaves)), key=lambda k: -leaves[k].size)
    width = (1, *leaves[order[0]].shape)[-1]
    lines = [
        jnp.pad(leaves[k].reshape(-1), (0, -leaves[k].size % width)).reshape(-1, width)
        for k in order
    ]
    both, at, found = (lax.all_gather(jnp.concatenate(lines), axis), 0, {})
    for k, line in zip(order, lines):
        section = both[:, at : at + len(line)].reshape(len(both), -1)
        found[k] = section[:, : leaves[k].size].reshape(-1, *leaves[k].shape)
        at += len(line)
    numbers = iter(range(len(leaves)))
    return jax.tree.map(lambda _: found[next(numbers)], array)


def merged_by_axis(array, axes, combine):
    for axis in axes:
        pieces = all_in_one(array, axis)
        array = jax.tree.map(lambda part: part[0], pieces)
        for k in range(1, lax.axis_size(axis)):
            array = combine(array, jax.tree.map(lambda part: part[k], pieces))
    return array


def in_blocks(array, dim, size):
    shape = array.shape
    pieces = array.reshape(*shape[:dim], size, shape[dim] // size, *shape[dim + 1 :])
    return jnp.moveaxis(pieces, dim, 0)


def one_exchange(array, axis, axes, splits, concats):
    sizes = [lax.axis_size(a) for a in axes]
    pieces = in_blocks(array, splits[0], sizes[0])
    pieces = jnp.moveaxis(in_blocks(pieces, splits[1] + 1, sizes[1]), 0, 1)
    inside = pieces.shape[2:]
    pieces = pieces.reshape(-1, *inside)
    pieces = lax.all_to_all(pieces, axis, split_axis=0, concat_axis=0, tiled=True)
    pieces = in_order(pieces.reshape(*sizes, *inside), concats[0] + 1)
    return in_order(pieces, concats[1])


def combine_pairs(earlier, later):
    new_max = jnp.maximum(earlier[0], later[0])
    new_sum = earlier[1] * jnp.exp(earlier[0] - new_max) + later[1] * jnp.exp(later[0] - new_max)
    return (new_max, new_sum)


def body(
    query,
    item_table,
    context_features,
    candidates,
    lengths,
    logged_slot,
    logging_prop,
    w_first,
    w_second,
    w_score,
):
    device_count = lax.axis_size(DP) * lax.axis_size(ITEM)
    item_rows = item_table.shape[0]
    width = item_table.shape[1]
    own_count = query.shape[0]
    slot_count = candidates.shape[1]
    gathered = gathered_by_axis(query, DP_ITEM, (2, 0, 3, 1), 0)
    context_total = gathered.shape[0]
    block_rows = min(512, item_rows)
    slabs = item_table.reshape(item_rows // block_rows, block_rows, width)

    def sweep(running, slab_rows):
        running_max, running_sum = running
        logits = lax.dot_general(
            gathered, slab_rows, (((1,), (1,)), ((), ())), preferred_element_type=jnp.float32
        )
        new_max = jnp.maximum(running_max, jnp.max(logits, axis=1))
        new_sum = running_sum * jnp.exp(running_max - new_max) + jnp.sum(
            jnp.exp(logits - new_max[:, None]), axis=1
        )
        return ((new_max, new_sum), None)

    initial = (
        jnp.full((context_total,), -1e30, jnp.float32),
        jnp.zeros((context_total,), jnp.float32),
    )
    (local_max, local_sum), unused_out = lax.scan(sweep, initial, slabs)
    first_context = lax.axis_index(DP_ITEM) * own_count
    global_max, global_sum = merged_by_axis((local_max, local_sum), DP_ITEM, combine_pairs)
    log_norm = lax.dynamic_slice_in_dim(global_max + jnp.log(global_sum), first_context, own_count)
    capacity = max(2, 3 * own_count * slot_count // (2 * device_count))
    flat_ids = candidates.reshape(-1)
    holder = flat_ids // item_rows
    same_holder = holder[:, None] == holder[None, :]
    earlier_slot = jnp.arange(flat_ids.shape[0])[None, :] < jnp.arange(flat_ids.shape[0])[:, None]
    holder_rank = jnp.sum((same_holder & earlier_slot).astype(jnp.int32), axis=1)
    bucket = holder * capacity + holder_rank
    outgoing = jnp.full((device_count * capacity,), -1, jnp.int32).at[bucket].set(flat_ids)
    outgoing = outgoing.reshape(lax.axis_size(DP), lax.axis_size(ITEM), capacity)
    first_item = lax.axis_index(DP_ITEM) * item_rows
    asked_ids = lax.all_to_all(
        lax.all_to_all(outgoing, ITEM, split_axis=1, concat_axis=1, tiled=True),
        DP,
        split_axis=0,
        concat_axis=0,
        tiled=True,
    )
    local_index = jnp.clip(asked_ids - first_item, 0, item_rows - 1)
    fetched = one_exchange(item_table[local_index], ITEM_DP, (ITEM, DP), (1, 0), (1, 0))
    cand_rows = fetched.reshape(device_count * capacity, width)[bucket]
    rows_by_context = cand_rows.reshape(own_count, slot_count, width)
    gen_logit = jnp.einsum("cd,ckd->ck", query, rows_by_context, preferred_element_type=jnp.float32)
    feature_width = context_features.shape[1]
    context_part = jnp.dot(
        context_features, w_first[:feature_width], preferred_element_type=jnp.float32
    )
    item_part = jnp.dot(cand_rows, w_first[feature_width:], preferred_element_type=jnp.float32)
    item_part = item_part.reshape(own_count, slot_count, -1)
    hidden = jax.nn.silu(item_part + context_part[:, None, :]).astype(jnp.bfloat16)
    hidden = hidden.reshape(own_count * slot_count, -1)
    second = jax.nn.silu(jnp.dot(hidden, w_second, preferred_element_type=jnp.float32)).astype(
        jnp.bfloat16
    )
    score = jnp.dot(second, w_score, preferred_element_type=jnp.float32).reshape(
        own_count, slot_count
    )
    positions = jnp.arange(slot_count, dtype=jnp.int32)
    live_slots = positions[None, :] < lengths[:, None]
    masked = jnp.where(live_slots, score, jnp.float32(-1e30))
    rank_peak = jnp.max(masked, axis=1)
    rank_norm = rank_peak + jnp.log(
        jnp.sum(
            jnp.where(live_slots, jnp.exp(masked - rank_peak[:, None]), jnp.float32(0.0)), axis=1
        )
    )
    total_items = item_rows * device_count
    section = jnp.where(
        live_slots,
        score - rank_norm[:, None] + gen_logit - log_norm[:, None] + math.log(total_items),
        jnp.float32(0.0),
    )
    chosen = jnp.sum(
        jnp.where(positions[None, :] == logged_slot[:, None], section, jnp.float32(0.0)), axis=1
    )
    log_weight = (
        chosen
        + jnp.log(lengths.astype(jnp.float32))
        - jnp.log(logging_prop.astype(jnp.float32) / 1024.0)
    )
    return (section, log_weight)


def solution(mesh):
    split = Mesh(mesh.devices.reshape(8, 2, 4, 8), ("dp_0", "dp_1", "item_0", "item_1"))
    placed = (
        P(DP_ITEM, None),
        P(DP_ITEM, None),
        P(DP_ITEM, None),
        P(DP_ITEM, None),
        P(DP_ITEM),
        P(DP_ITEM),
        P(DP_ITEM),
        P(),
        P(),
        P(),
    )
    return jax.shard_map(
        body, mesh=split, in_specs=placed, out_specs=(P(DP_ITEM, None), P(DP_ITEM)), check_vma=False
    )
```

profile of v0, /device:TPU:44, one launch (start us, length us, event | category | flops | bytes accessed | tf_op | source)
XLA Modules:
  0.0 200.7 jit_solution(16794358863279650600)
XLA Ops:
  0.6 0.0 copy-start
  0.6 0.8 and_select_fusion
  1.4 0.7 add_select_fusion
  2.1 0.5 convert_reduce_fusion
  2.6 0.7 compare_select_fusion.1
  3.4 4.5 %scatter_custom_fusion = s32[1536]{0:T(1024)S(1)} fusion(s32[1024]{0:T(1024)S(1)} %bitcast.356, s32[1024]{0:T(1024)} %bitcast.354, s32[]{:T(128)} %constant.34.clone.1), kind=kCustom, calls=%fused_computation.48 | custom fusion | bytes 6656 | tf_op jit(solution)/shard_map/scatter | solution.py:132
  7.8 0.2 reshape.895
  8.1 0.0 copy-start.1
  8.1 0.9 copy.25
  9.0 13.4 %all-to-all-start = ((s32[16,32,3]{0,2,1:T(4,128)}), s32[16,32,3]{0,2,1:T(4,128)S(1)}, u32[]{:S(2)}, u32[]{:S(2)}) async-start(s32[16,32,3]{0,2,1:T(4,128)} %copy.25), calls=%async_computation | async-start | bytes 131072 | tf_op jit(solution)/shard_map/all_to_all | solution.py:136
  22.4 7.8 %all-gather.8 = bf16[4,1,256]{2,1,0:T(2,128)(2,1)S(1)} all-gather(bf16[1,1,256]{2,1,0:T(2,128)(2,1)} %bitcast.375), channel_id=2, replica_groups=mesh['dp_0'=8,'dp_1'=2,'item_0'=4,'item_1'=8] {'item_0'}, dimensions={0}, use_global_device_ids=true | all-gather | bytes 2560 | tf_op jit(solution)/shard_map/all_gather | solution.py:24
  30.2 20.8 %all-gather.9 = bf16[8,4,256]{2,1,0:T(4,128)(2,1)S(1)} all-gather(bf16[1,4,256]{2,1,0:T(4,128)(2,1)S(1)} %bitcast.374), channel_id=3, replica_groups=mesh['dp_0'=8,'dp_1'=2,'item_0'=4,'item_1'=8] {'dp_0'}, dimensions={0}, use_global_device_ids=true | all-gather | bytes 18432 | tf_op jit(solution)/shard_map/all_gather | solution.py:24
  51.0 25.5 %all-gather.2 = bf16[256,256]{1,0:T(8,128)(2,1)S(1)} all-gather(bf16[32,256]{1,0:T(8,128)(2,1)S(1)} %reshape.943), channel_id=4, replica_groups=mesh['dp_0'=8,'dp_1'=2,'item_0'=4,'item_1'=8] {'item_1'}, dimensions={0}, use_global_device_ids=true | all-gather | bytes 147456 | tf_op jit(solution)/shard_map/all_gather | solution.py:24
  76.6 2.0 all-gather.3
  78.5 0.1 reshape.901
  78.6 0.1 copy.32
  78.8 0.0 copy-done.1
  78.8 0.0 copy-start.5
  78.8 2.4 %while.13 = (s32[]{:T(128)}, f32[512]{0:T(512)S(1)}, f32[512]{0:T(512)S(1)}, bf16[4,512,256]{2,1,0:T(8,128)(2,1)S(1)}, bf16[512,256]{1,0:T(8,128)(2,1)S(1)}, /*index=5*/s32[]{:T(128)}, s32[]{:T(128)}) while((s32[]{:T(128)}, f32[512]{0:T(512)S(1)}, f32[512]{0:T(512)S(1)}, bf16[4,512,256]{2,1,0:T(8,128)(2,1)S(1)}, ...), condition=%wide.region_7.8_spmd.clone, body=%wide.region_4.7_spmd.clone.sunk | while | flops 135006720 | bytes 2648156 | solution.py:121
  78.8 0.3 fusion.97
  79.2 0.2 exponential_reduce_fusion.2
  79.4 0.3 fusion.97
  79.8 0.2 exponential_reduce_fusion.2
  80.0 0.3 fusion.97
  80.4 0.2 exponential_reduce_fusion.2
  80.6 0.3 fusion.97
  80.9 0.2 exponential_reduce_fusion.2
  81.2 23.3 %all-gather.10 = f32[8,2,512]{2,1,0:T(2,128)S(1)} all-gather(f32[1,2,512]{2,1,0:T(2,128)S(1)} %maximum_bitcast_fusion), channel_id=6, replica_groups=mesh['dp_0'=8,'dp_1'=2,'item_0'=4,'item_1'=8] {'dp_0'}, dimensions={0}, use_global_device_ids=true | all-gather | bytes 36864 | tf_op jit(solution)/shard_map/all_gather | solution.py:43
  104.4 0.1 fusion.32
  104.5 0.0 all-to-all-done
  104.5 0.7 copy.26
  105.2 8.3 %all-to-all-start.1 = ((s32[16,32,3]{1,2,0:T(4,128)}), s32[16,32,3]{1,2,0:T(4,128)S(1)}, u32[]{:S(2)}, u32[]{:S(2)}) async-start(s32[16,32,3]{1,2,0:T(4,128)} %copy.26), calls=%async_computation.1 | async-start | bytes 65536 | tf_op jit(solution)/shard_map/all_to_all | solution.py:135
  113.5 0.0 copy-done.5
  115.6 1.8 all-gather.11
  117.4 0.0 all-to-all-done.1
  117.4 0.2 copy.27
  117.6 0.2 reshape.906
  117.8 4.8 %gather_fusion = bf16[1536,256]{1,0:T(8,128)(2,1)S(1)} fusion(bf16[2048,256]{1,0:T(8,128)(2,1)S(1)} %bitcast.342, s32[2048]{0:T(1024)S(1)} %pad_clamp_fusion), kind=kCustom, calls=%fused_computation | custom fusion | bytes 1579008 | tf_op jit(solution)/shard_map/gather | solution.py:143
  122.6 0.4 reshape.896
  123.0 0.6 copy.28
  123.6 1.7 copy.29
  125.2 0.0 copy-start.2
  125.2 0.0 copy-start.4
  125.2 16.4 %all-to-all-start.2 = ((bf16[512,1,1,3,256]{4,3,2,1,0:T(4,128)(2,1)}), bf16[512,1,1,3,256]{4,3,2,1,0:T(4,128)(2,1)S(1)}, u32[]{:S(2)}, u32[]{:S(2)}) async-start(bf16[512,1,1,3,256]{4,3,2,1,0:T(4,128)(2,1)} %copy.29), calls=%async_computation.2 | async-start | bytes 2097152 | tf_op jit(solution)/shard_map/all_to_all | solution.py:73
  141.6 10.8 %all-gather.12 = f32[4,2,512]{2,1,0:T(2,128)S(1)} all-gather(f32[1,2,512]{2,1,0:T(2,128)S(1)} %maximum_bitcast_fusion.2), channel_id=8, replica_groups=mesh['dp_0'=8,'dp_1'=2,'item_0'=4,'item_1'=8] {'item_0'}, dimensions={0}, use_global_device_ids=true | all-gather | bytes 20480 | tf_op jit(solution)/shard_map/all_gather | solution.py:43
  152.4 32.8 %all-gather.13 = f32[8,2,512]{2,1,0:T(2,128)S(1)} all-gather(f32[1,2,512]{2,1,0:T(2,128)S(1)} %maximum_bitcast_fusion.3), channel_id=9, replica_groups=mesh['dp_0'=8,'dp_1'=2,'item_0'=4,'item_1'=8] {'item_1'}, dimensions={0}, use_global_device_ids=true | all-gather | bytes 36864 | tf_op jit(solution)/shard_map/all_gather | solution.py:43
  185.4 0.6 dynamic_slice.7
  185.9 0.0 copy-done.2
  185.9 0.0 copy-done.4
  186.0 0.2 fusion.9
  186.1 0.0 all-to-all-done.2
  186.1 0.1 copy.30
  186.3 0.7 copy.31
  186.9 0.7 reshape_reshape_reshape.3
  187.6 0.0 copy-start.3
  187.7 3.9 %gather_fusion.1 = bf16[1024,256]{1,0:T(8,128)(2,1)S(1)} fusion(bf16[1536,256]{1,0:T(8,128)(2,1)S(1)} %reshape_reshape_reshape.3, s32[1024]{0:T(1024)S(1)} %broadcast_clamp_fusion), kind=kCustom, calls=%fused_computation.1 | custom fusion | bytes 1052672 | tf_op jit(solution)/shard_map/gather | solution.py:144
  191.6 0.0 copy-done.3
  191.6 0.2 fusion.78
  191.8 0.0 copy-done
  191.9 1.4 multiply_convert_fusion
  193.3 0.4 fusion.86
  193.7 0.6 fusion.18
  194.3 1.3 select_reduce_fusion.1
  197.0 1.8 select_reduce_fusion
  (28 shorter events, 0.3 us)
Async XLA Ops:
  0.6 191.2 %copy-start = (bf16[512,512]{1,0:T(8,128)(2,1)S(1)}, bf16[512,512]{1,0:T(8,128)(2,1)}, u32[]{:S(2)}) copy-start(bf16[512,512]{1,0:T(8,128)(2,1)} %param.20) | copy-start | bytes 1572868
  8.1 70.7 %copy-start.1 = (bf16[2048,256]{1,0:T(8,128)(2,1)S(1)}, bf16[2048,256]{1,0:T(8,128)(2,1)}, u32[]{:S(2)}) copy-start(bf16[2048,256]{1,0:T(8,128)(2,1)} %param.13) | copy-start | bytes 3145732
  9.0 95.5 %all-to-all-start = ((s32[16,32,3]{0,2,1:T(4,128)}), s32[16,32,3]{0,2,1:T(4,128)S(1)}, u32[]{:S(2)}, u32[]{:S(2)}) async-start(s32[16,32,3]{0,2,1:T(4,128)} %copy.25), calls=%async_computation | async-start | bytes 131072 | tf_op jit(solution)/shard_map/all_to_all | solution.py:136
  78.8 34.8 %copy-start.5 = (bf16[512]{0:T(512)(128)(2,1)S(1)}, bf16[512]{0:T(512)(128)(2,1)}, u32[]{:S(2)}) copy-start(bf16[512]{0:T(512)(128)(2,1)} %param.21) | copy-start | bytes 3076
  105.2 12.2 %all-to-all-start.1 = ((s32[16,32,3]{1,2,0:T(4,128)}), s32[16,32,3]{1,2,0:T(4,128)S(1)}, u32[]{:S(2)}, u32[]{:S(2)}) async-start(s32[16,32,3]{1,2,0:T(4,128)} %copy.26), calls=%async_computation.1 | async-start | bytes 65536 | tf_op jit(solution)/shard_map/all_to_all | solution.py:135
  125.2 60.7 %copy-start.2 = (bf16[768,512]{1,0:T(8,128)(2,1)S(1)}, bf16[768,512]{1,0:T(8,128)(2,1)}, u32[]{:S(2)}) copy-start(bf16[768,512]{1,0:T(8,128)(2,1)} %param.19) | copy-start | bytes 2359300
  125.2 60.7 %copy-start.4 = (bf16[1,512]{1,0:T(2,128)(2,1)S(1)}, bf16[1,512]{1,0:T(2,128)(2,1)}, u32[]{:S(2)}) copy-start(bf16[1,512]{1,0:T(2,128)(2,1)} %param.14) | copy-start | bytes 3076
  125.2 60.9 %all-to-all-start.2 = ((bf16[512,1,1,3,256]{4,3,2,1,0:T(4,128)(2,1)}), bf16[512,1,1,3,256]{4,3,2,1,0:T(4,128)(2,1)S(1)}, u32[]{:S(2)}, u32[]{:S(2)}) async-start(bf16[512,1,1,3,256]{4,3,2,1,0:T(4,128)(2,1)} %copy.29), calls=%async_computation.2 | async-start | bytes 2097152 | tf_op jit(solution)/shard_map/all_to_all | solution.py:73
  187.6 4.0 %copy-start.3 = (bf16[1,256]{1,0:T(2,128)(2,1)S(1)}, bf16[1,256]{1,0:T(2,128)(2,1)}, u32[]{:S(2)}) copy-start(bf16[1,256]{1,0:T(2,128)(2,1)} %param.12) | copy-start | bytes 1540
where the time goes:
time: 201 us
  blocking collectives  125 us (62%)
  starting transfers between devices  38.1 us (19%)
  local copies, waits for them, and re-layouts  20.4 us (10%)
  other arithmetic  7.58 us (4%)
  between operations  6.14 us (3%)
  matrix products  3.57 us (2%)
    all_gather x4, blocking collectives, all_in_one(): both, at, found = (lax.all_gather(jnp.concatenate(lines), axis), 0, {})  68.7 us
    all_gather x4, blocking collectives, stacked_from(): pieces = lax.all_gather(pieces, axes[k], axis=0, tiled=True)  56.1 us
    all_to_all x1, starting transfers between devices, one_exchange(): lax.all_to_all(pieces, axis, split_axis=0, concat_axis=0, tiled=True)  16.4 us
    all_to_all x1, starting transfers between devices, body(): lax.all_to_all(outgoing, ITEM, split_axis=1, concat_axis=1, tiled=True)  13.4 us
    all_to_all x1, starting transfers between devices, body(): lax.all_to_all(lax.all_to_all(outgoing, ITEM, split_axis=1, concat_axis=1...  8.31 us
    gather x1, local copies, waits for them, and re-layouts, body(): item_table[local_index]  4.76 us
    scatter x1, local copies, waits for them, and re-layouts, body(): jnp.full((device_count * capacity,), -1, jnp.int32).at[bucket].set(flat_ids)  4.48 us
  transfers between devices with their start and end apart: 3, of which 0 were waited for; matrix products, arithmetic and copies ran while one was open for 2% of the time, Pallas kernels for 0%

commit v1 on v0

v1 whole, which is shorter than its diff:
```python
import math

import jax
import jax.numpy as jnp
from jax import lax
from jax.experimental import pallas as pl
from jax.experimental.pallas import tpu as pltpu
from jax.sharding import Mesh
from jax.sharding import PartitionSpec as P

ALL = ("y", "core", "x", "z")
CHIPS = ("y", "x", "z")
BIG = 1 << 24
CAP = 3
BF = jnp.bfloat16
F32 = jnp.float32


def dot_nt(a, b):
    return lax.dot_general(a, b, (((1,), (1,)), ((), ())), preferred_element_type=F32)


def dot_nn(a, b):
    return lax.dot_general(a, b, (((1,), (0,)), ((), ())), preferred_element_type=F32)


def silu(v):
    half = 0.5 * v
    return half + half * jnp.tanh(half)


def ask_kernel(plane, chips, item_rows, query_ref, feature_ref, ids_ref, payload_ref, pick_ref):
    slots = ids_ref.shape[1]
    ids = ids_ref[...]
    holder = ids // item_rows
    local = ids % item_rows
    slot = lax.broadcasted_iota(jnp.int32, ids.shape, 1)
    key = slot * item_rows + local
    chip = lax.broadcasted_iota(jnp.int32, (chips, 1), 0)
    lane = lax.broadcasted_iota(jnp.int32, (chips, 256), 1)
    asked = jnp.zeros((chips, 256), F32)
    first = jnp.zeros((1, slots), jnp.int32)
    last = jnp.zeros((1, slots), jnp.int32)
    for core in range(2):
        device = (chip // plane) * (2 * plane) + core * plane + chip % plane
        mine = holder == device
        low = jnp.min(jnp.where(mine, key, BIG), axis=1, keepdims=True)
        high = jnp.max(jnp.where(mine, key, -1), axis=1, keepdims=True)
        total = jnp.sum(jnp.where(mine, key, 0), axis=1, keepdims=True)
        middle = total - low - high
        have = (high >= 0, (high > low) & (middle > 0), high > low)
        for j, (wanted, ok) in enumerate(zip((low, middle, high), have)):
            inside = jnp.where(ok, wanted % item_rows, 2 * item_rows)
            place = 2 * (core * CAP + j)
            asked = jnp.where(lane == place, (inside // 256).astype(F32), asked)
            asked = jnp.where(lane == place + 1, (inside % 256).astype(F32), asked)
        first = first + jnp.sum(jnp.where(low == key, 1, 0), axis=0, keepdims=True)
        last = last + jnp.sum(jnp.where(high == key, 1, 0), axis=0, keepdims=True)
    width = query_ref.shape[1]
    feature_width = feature_ref.shape[1]
    payload_ref[:, :width] = jnp.broadcast_to(query_ref[...], (chips, width))
    payload_ref[:, width : width + feature_width] = jnp.broadcast_to(
        feature_ref[...], (chips, feature_width)
    )
    payload_ref[:, width + feature_width :] = asked.astype(BF)
    place = jnp.where(first > 0, 0, jnp.where(last > 0, 2, 1))
    pick_ref[...] = ((holder // plane) % 2) * CAP + place


def hold_kernel(asked_ref, table_ref, w_first_ref, w_second_ref, w_score_ref, out_ref, logits_ref):
    contexts = asked_ref.shape[0]
    width = table_ref.shape[2]
    item_rows = table_ref.shape[1]
    feature_width = w_first_ref.shape[0] - width
    query = asked_ref[:, :width]
    lane = lax.broadcasted_iota(jnp.int32, (contexts, 128), 1)
    chunk = 512
    peak = jnp.full((contexts, 128), -1e30, F32)
    for core in range(2):
        for start in range(0, item_rows, chunk):
            logits = dot_nt(query, table_ref[core, start : start + chunk, :])
            at = core * item_rows + start
            logits_ref[:, at : at + chunk] = logits
            for k in range(0, chunk, 128):
                peak = jnp.maximum(peak, logits[:, k : k + 128])
    peak = jnp.max(peak, axis=1, keepdims=True)
    total = jnp.zeros((contexts, 128), F32)
    for start in range(0, 2 * item_rows, 128):
        total = total + jnp.exp(logits_ref[:, start : start + 128] - peak)
    total = jnp.sum(total, axis=1, keepdims=True)
    out = jnp.where(lane == 4 * CAP, peak, jnp.where(lane == 4 * CAP + 1, total, 0.0))

    context_part = dot_nn(
        asked_ref[:, width : width + feature_width], w_first_ref[:feature_width, :]
    )
    query_wide = query.astype(F32)
    id_parts = asked_ref[:, width + feature_width :].astype(F32)
    item = lax.broadcasted_iota(jnp.int32, (contexts, item_rows), 1)
    w_score = jnp.broadcast_to(w_score_ref[...], (128, w_score_ref.shape[1]))
    for core in range(2):
        for j in range(CAP):
            place = core * CAP + j
            inside = id_parts[:, 2 * place : 2 * place + 1] * 256.0
            inside = (inside + id_parts[:, 2 * place + 1 : 2 * place + 2]).astype(jnp.int32)
            chosen = jnp.where(item == inside, 1.0, 0.0).astype(BF)
            rows = dot_nn(chosen, table_ref[core])
            gen = jnp.sum(rows * query_wide, axis=1, keepdims=True)
            hidden = silu(dot_nn(rows.astype(BF), w_first_ref[feature_width:, :]) + context_part)
            second = silu(dot_nn(hidden.astype(BF), w_second_ref[...]))
            score = dot_nt(second.astype(BF), w_score)
            out = jnp.where(lane == place, score, out)
            out = jnp.where(lane == 2 * CAP + place, gen, out)
    out_ref[...] = out


def own_kernel(
    plane, item_rows, total_items,
    back_ref, ids_ref, pick_ref, length_ref, logged_ref, prop_ref, section_ref, weight_ref,
):
    chips = back_ref.shape[0]
    slots = ids_ref.shape[1]
    back = jnp.transpose(back_ref[...])[:16]
    peaks, sums = back[4 * CAP : 4 * CAP + 1], back[4 * CAP + 1 : 4 * CAP + 2]
    peak = jnp.max(peaks, axis=1, keepdims=True)
    log_norm = peak + jnp.log(jnp.sum(sums * jnp.exp(peaks - peak), axis=1, keepdims=True))
    holder = ids_ref[...] // item_rows
    chip_of = (holder // (2 * plane)) * plane + holder % plane
    chip = lax.broadcasted_iota(jnp.int32, (chips, slots), 0)
    chosen = jnp.where(chip == chip_of, 1.0, 0.0).astype(BF)
    top = back.astype(BF)
    rest = back - top.astype(F32)
    middle = rest.astype(BF)
    low = (rest - middle.astype(F32)).astype(BF)
    found = dot_nn(top, chosen) + dot_nn(middle, chosen) + dot_nn(low, chosen)
    pick = pick_ref[...]
    score = jnp.zeros((1, slots), F32)
    gen = jnp.zeros((1, slots), F32)
    for place in range(2 * CAP):
        score = jnp.where(pick == place, found[place : place + 1], score)
        gen = jnp.where(pick == place, found[2 * CAP + place : 2 * CAP + place + 1], gen)
    slot = lax.broadcasted_iota(jnp.int32, (1, slots), 1)
    length = length_ref[0]
    live = slot < length
    masked = jnp.where(live, score, -1e30)
    rank_peak = jnp.max(masked, axis=1, keepdims=True)
    rank_sum = jnp.sum(jnp.where(live, jnp.exp(masked - rank_peak), 0.0), axis=1, keepdims=True)
    rank_norm = rank_peak + jnp.log(rank_sum)
    section = jnp.where(live, score - rank_norm + gen - log_norm + math.log(total_items), 0.0)
    section_ref[...] = section
    chosen = jnp.sum(jnp.where(slot == logged_ref[0], section, 0.0), axis=1, keepdims=True)
    ones = jnp.ones((1, 128), F32)
    weight_ref[...] = (
        chosen
        + jnp.log(ones * length.astype(F32))
        - jnp.log(ones * (prop_ref[0].astype(F32) / 1024.0))
    )


def body(
    query, item_table, context_features, candidates, lengths, logged_slot, logging_prop,
    w_first, w_second, w_score,
):
    item_rows, width = item_table.shape
    slots = candidates.shape[1]
    feature_width = context_features.shape[1]
    chips = lax.axis_size(CHIPS)
    plane = lax.axis_size(("x", "z"))
    message = width + feature_width + 256
    vmem = pl.BlockSpec(memory_space=pltpu.VMEM)
    smem = pl.BlockSpec(memory_space=pltpu.SMEM)

    tables = lax.all_gather(item_table, "core", axis=0, tiled=False)
    payload, pick = pl.pallas_call(
        lambda *refs: ask_kernel(plane, chips, item_rows, *refs),
        out_shape=(
            jax.ShapeDtypeStruct((chips, message), BF),
            jax.ShapeDtypeStruct((1, slots), jnp.int32),
        ),
        in_specs=[vmem] * 3,
        out_specs=(vmem, vmem),
        name="ask",
    )(query, context_features, candidates)
    asked = lax.all_to_all(
        payload.reshape(chips, message // 128, 128), CHIPS, split_axis=0, concat_axis=0, tiled=True
    ).reshape(chips, message)
    answers = pl.pallas_call(
        hold_kernel,
        out_shape=jax.ShapeDtypeStruct((chips, 128), F32),
        in_specs=[vmem] * 5,
        out_specs=vmem,
        scratch_shapes=[pltpu.VMEM((chips, 2 * item_rows), F32)],
        compiler_params=pltpu.CompilerParams(vmem_limit_bytes=40 * 1024 * 1024),
        name="hold",
    )(asked, tables, w_first, w_second, w_score.reshape(1, -1))
    back = lax.all_to_all(
        answers.reshape(chips, 1, 128), CHIPS, split_axis=0, concat_axis=0, tiled=True
    ).reshape(chips, 128)
    total_items = item_rows * 2 * chips
    section, weight = pl.pallas_call(
        lambda *refs: own_kernel(plane, item_rows, total_items, *refs),
        out_shape=(
            jax.ShapeDtypeStruct((1, slots), F32),
            jax.ShapeDtypeStruct((1, 128), F32),
        ),
        in_specs=[vmem] * 3 + [smem] * 3,
        out_specs=(vmem, vmem),
        name="own",
    )(back, candidates, pick, lengths, logged_slot, logging_prop)
    return section, weight[0, :1]


def solution(mesh):
    split = Mesh(mesh.devices.reshape(8, 2, 4, 8), ALL)
    row, flat = P(ALL, None), P(ALL)
    placed = (row, row, row, row, flat, flat, flat, P(), P(), P())
    return jax.shard_map(
        body, mesh=split, in_specs=placed, out_specs=(row, flat), check_vma=False
    )
```

time: 201 us -> 96 us (0.48)
  the two profiles are of different devices: /device:TPU:44 before, /device:TPU:1 now
where the time goes in v1:
time: 96 us; the launch traced here: 94.8 us
  starting transfers between devices  33 us (34%)
  waiting for transfers between devices  29.6 us (31%)
  between operations  16.1 us (17%)
  Pallas kernels  11.9 us (12%)
  local copies, waits for them, and re-layouts  4.29 us (4%)
    all_to_all x1, starting transfers between devices, body(): lax.all_to_all(payload.reshape(chips, message // 128, 128), CHIPS, split_...  23.4 us
    all_to_all x1, waiting for transfers between devices, body(): lax.all_to_all(payload.reshape(chips, message // 128, 128), CHIPS, split_...  18.7 us
    all_to_all x1, waiting for transfers between devices, body(): lax.all_to_all(answers.reshape(chips, 1, 128), CHIPS, split_axis=0, conca...  10.2 us
    all_to_all x1, starting transfers between devices, body(): lax.all_to_all(answers.reshape(chips, 1, 128), CHIPS, split_axis=0, conca...  9.55 us
    pallas_call x1, Pallas kernels, body(): pl.pallas_call(hold_kernel, out_shape=jax.ShapeDtypeStruct((chips, 128),...  5.96 us
    unnamed x12, local copies, waits for them, and re-layouts  4.29 us
    pallas_call x1, Pallas kernels, body(): pl.pallas_call(lambda *refs: ask_kernel(plane, chips, item_rows, *refs),...  3.8 us
    pallas_call x1, Pallas kernels, body(): pl.pallas_call(lambda *refs: own_kernel(plane, item_rows, total_items, *r...  2.16 us
  transfers between devices with their start and end apart: 3, of which 2 were waited for; matrix products, arithmetic and copies ran while one was open for 2% of the time, Pallas kernels for 4%

profile of v1, /device:TPU:1, one launch (start us, length us, event | category | flops | bytes accessed | tf_op | source)
XLA Modules:
  0.0 94.8 jit_solution(6007050785063599161)
XLA Ops:
  7.2 0.0 copy-start.4
  7.2 0.0 copy-start.1
  7.2 0.0 copy-start.2
  7.2 0.0 all-gather.3.cloned.1.call-start
  7.2 0.7 all-gather.3.cloned.1.call-update
  7.9 3.8 %ask.1 = (bf16[256,1024]{1,0:T(8,128)(2,1)}, s32[1,1024]{1,0:T(1,128)}) custom-call(bf16[1,256]{1,0:T(2,128)(2,1)} %refs_0_.1, bf16[1,512]{1,0:T(2,128)(2,1)} %refs_1_.2, s32[1,1024]{1,0:T(1,128)} %refs_1_.3), custom_call_target="tpu_custom_call" | custom-call | tf_op jit(solution)/shard_map/ask/pallas_call | solution.py:173
  11.7 1.9 %copy.13 = bf16[32,8,8,128]{3,2,1,0:T(8,128)(2,1)} copy(bf16[32,8,8,128]{3,1,2,0:T(8,128)(2,1)} %bitcast.16) | data formatting | bytes 1048576
  13.7 23.4 %all-to-all-start = ((bf16[256,8,128]{2,1,0:T(8,128)(2,1)}), bf16[256,8,128]{2,1,0:T(8,128)(2,1)S(1)}, u32[]{:S(2)}, u32[]{:S(2)}) async-start(bf16[256,8,128]{2,1,0:T(8,128)(2,1)} %bitcast.7), calls=%async_computation | async-start | bytes 1048576 | tf_op jit(solution)/shard_map/all_to_all | solution.py:183
  37.1 0.0 copy-done.4
  37.1 18.7 %all-to-all-done = bf16[256,8,128]{2,1,0:T(8,128)(2,1)S(1)} async-done(((bf16[256,8,128]{2,1,0:T(8,128)(2,1)}), bf16[256,8,128]{2,1,0:T(8,128)(2,1)S(1)}, u32[]{:S(2)}, u32[]{:S(2)}) %all-to-all-start) | async-done | bytes 524320 | tf_op jit(solution)/shard_map/all_to_all | solution.py:183
  55.7 0.1 copy.16
  55.9 0.0 all-gather.3.cloned.1.call-done
  55.9 0.0 copy-done.1
  55.9 0.0 copy-done.2
  55.9 0.0 copy-start
  55.9 1.6 %copy-done = bf16[4096,256]{1,0:T(8,128)(2,1)S(1)} copy-done((bf16[4096,256]{1,0:T(8,128)(2,1)S(1)}, bf16[4096,256]{1,0:T(8,128)(2,1)}, u32[]{:S(2)}) %copy-start) | copy-done | bytes 2097176
  57.5 6.0 %hold.1 = f32[256,128]{1,0:T(8,128)} custom-call(bf16[256,1024]{1,0:T(8,128)(2,1)S(1)} %bitcast.14, bf16[2,2048,256]{2,1,0:T(8,128)(2,1)S(1)} %bitcast.13, bf16[768,512]{1,0:T(8,128)(2,1)S(1)} %copy-done.1, bf16[512,512]{1,0:T(8,128)(2,1)S(1)} %copy-done.2, bf16[1,512]{1,0:T(2,128)(2,1)S(1)} %reshape.21.w_score_ref), custom_call_target="tpu_custom_call" | custom-call | tf_op jit(solution)/shard_map/hold/pallas_call | solution.py:186
  63.4 9.6 %all-to-all-start.1 = ((f32[256,1,128]{2,1,0:T(1,128)}), f32[256,1,128]{2,1,0:T(1,128)S(1)}, u32[]{:S(2)}, u32[]{:S(2)}) async-start(f32[256,1,128]{2,1,0:T(1,128)} %bitcast.2), calls=%async_computation.1 | async-start | bytes 262144 | tf_op jit(solution)/shard_map/all_to_all | solution.py:195
  74.9 10.2 %all-to-all-done.1 = f32[256,1,128]{2,1,0:T(1,128)S(1)} async-done(((f32[256,1,128]{2,1,0:T(1,128)}), f32[256,1,128]{2,1,0:T(1,128)S(1)}, u32[]{:S(2)}, u32[]{:S(2)}) %all-to-all-start.1) | async-done | bytes 131104 | tf_op jit(solution)/shard_map/all_to_all | solution.py:195
  85.2 0.0 copy-start.3
  85.2 0.6 copy-done.3
  85.8 2.2 %own.1 = (f32[1,1024]{1,0:T(1,128)}, f32[1,128]{1,0:T(1,128)}) custom-call(f32[256,128]{1,0:T(8,128)} %bitcast.17, s32[1,1024]{1,0:T(1,128)} %refs_1_.3, s32[1,1024]{1,0:T(1,128)} %get-tuple-element.7.refs_2_, s32[1]{0:T(128)S(6)} %copy.17.refs_3_, s32[1]{0:T(128)S(6)} %copy.18.refs_4_, s32[1]{0:T(128)S(6)} %copy.19.refs_5_), custom_call_target="tpu_custom_call" | custom-call | tf_op jit(solution)/shard_map/own/pallas_call | solution.py:199
  (1 shorter events, 0.0 us)
Async XLA Ops:
  7.2 29.9 %copy-start.4 = (bf16[512]{0:T(512)(128)(2,1)S(1)}, bf16[512]{0:T(512)(128)(2,1)}, u32[]{:S(2)}) copy-start(bf16[512]{0:T(512)(128)(2,1)} %param.19) | copy-start | bytes 3076
  7.2 48.7 %copy-start.1 = (bf16[768,512]{1,0:T(8,128)(2,1)S(1)}, bf16[768,512]{1,0:T(8,128)(2,1)}, u32[]{:S(2)}) copy-start(bf16[768,512]{1,0:T(8,128)(2,1)} %w_first_ref.1) | copy-start | bytes 2359300
  7.2 48.7 %copy-start.2 = (bf16[512,512]{1,0:T(8,128)(2,1)S(1)}, bf16[512,512]{1,0:T(8,128)(2,1)}, u32[]{:S(2)}) copy-start(bf16[512,512]{1,0:T(8,128)(2,1)} %w_second_ref.1) | copy-start | bytes 1572868
  7.2 48.7 %all-gather.3.cloned.1.call-start = ((), (), s32[]{:S(2)}) async-start(), calls=%async_computation.2 | async-start | bytes 3145728 | tf_op jit(solution)/shard_map/all_gather | solution.py:172
  13.7 42.1 %all-to-all-start = ((bf16[256,8,128]{2,1,0:T(8,128)(2,1)}), bf16[256,8,128]{2,1,0:T(8,128)(2,1)S(1)}, u32[]{:S(2)}, u32[]{:S(2)}) async-start(bf16[256,8,128]{2,1,0:T(8,128)(2,1)} %bitcast.7), calls=%async_computation | async-start | bytes 1048576 | tf_op jit(solution)/shard_map/all_to_all | solution.py:183
  55.9 1.6 %copy-start = (bf16[4096,256]{1,0:T(8,128)(2,1)S(1)}, bf16[4096,256]{1,0:T(8,128)(2,1)}, u32[]{:S(2)}) copy-start(bf16[4096,256]{1,0:T(8,128)(2,1)} %all-gather.3.cloned.1.call-done) | copy-start | bytes 6291460
  63.4 21.7 %all-to-all-start.1 = ((f32[256,1,128]{2,1,0:T(1,128)}), f32[256,1,128]{2,1,0:T(1,128)S(1)}, u32[]{:S(2)}, u32[]{:S(2)}) async-start(f32[256,1,128]{2,1,0:T(1,128)} %bitcast.2), calls=%async_computation.1 | async-start | bytes 262144 | tf_op jit(solution)/shard_map/all_to_all | solution.py:195
  85.2 0.7 copy-start.3
Sparse Core Ops, SparseCore 0:
  10.1 25.6 all-gather.2

commit v2 on v1

v2 whole, which is shorter than its diff:
```python
import math

import jax
import jax.numpy as jnp
from jax import lax
from jax.experimental import pallas as pl
from jax.experimental.pallas import tpu as pltpu
from jax.sharding import Mesh
from jax.sharding import PartitionSpec as P

ALL = ("y", "core", "x", "z")
CHIPS = ("y", "x", "z")
BIG = float(1 << 24)
CAP = 3
ROWS = 8
BF = jnp.bfloat16
F32 = jnp.float32


def dot_nt(a, b):
    return lax.dot_general(a, b, (((1,), (1,)), ((), ())), preferred_element_type=F32)


def dot_nn(a, b):
    return lax.dot_general(a, b, (((1,), (0,)), ((), ())), preferred_element_type=F32)


def silu(v):
    half = 0.5 * v
    return half + half * jnp.tanh(half)


def asked_keys(which, plane, chips, item_rows, ids):
    holder = lax.shift_right_logical(ids, item_rows.bit_length() - 1)
    slot = lax.broadcasted_iota(jnp.int32, ids.shape, 1)
    key = (slot * item_rows + (ids & (item_rows - 1))).astype(F32)
    core = lax.axis_index("core") ^ which
    chip = lax.broadcasted_iota(jnp.int32, (chips, 1), 0)
    device = (chip // plane) * (2 * plane) + core * plane + chip % plane
    mine = holder == device
    low = jnp.min(jnp.where(mine, key, BIG), axis=1, keepdims=True)
    high = jnp.max(jnp.where(mine, key, -1.0), axis=1, keepdims=True)
    total = jnp.sum(jnp.where(mine, key, 0.0), axis=1, keepdims=True)
    return key, low, high, total


def ask_kernel(plane, chips, item_rows, query_ref, feature_ref, ids_ref, message_ref):
    ids = ids_ref[...]
    lane = lax.broadcasted_iota(jnp.int32, (chips, 128), 1)
    wanted = jnp.full((chips, 128), -1.0, F32)
    for which in range(2):
        _, low, high, total = asked_keys(which, plane, chips, item_rows, ids)
        middle = total - low - high
        least = jnp.where(high >= 0.0, low, -1.0)
        middle = jnp.where((high > low) & (middle > 0.0), middle, -1.0)
        most = jnp.where(high > low, high, -1.0)
        for j, keys in enumerate((least, middle, most)):
            at = 2 * (which * CAP + j)
            wanted = jnp.where((lane == at) | (lane == at + 1), keys, wanted)
    wanted = wanted.astype(jnp.int32)
    inside = jnp.where(wanted < 0, 2 * item_rows, wanted & (item_rows - 1))
    asked = jnp.where((lane & 1) == 0, lax.shift_right_logical(inside, 8), inside & 255)
    asked = asked.astype(F32).astype(BF)
    row = lax.broadcasted_iota(jnp.int32, (ROWS * chips, chips), 0)
    chip = lax.broadcasted_iota(jnp.int32, (ROWS * chips, chips), 1)
    spread = jnp.where(row == chip * ROWS + ROWS - 2, 1.0, 0.0).astype(BF)
    spread = dot_nn(spread, asked).reshape(chips, ROWS, 128)
    line = lax.broadcasted_iota(jnp.int32, (ROWS, 128), 0)
    own = jnp.zeros((ROWS, 128), F32)
    at = 0
    for ref in (query_ref, feature_ref):
        for k in range(0, ref.shape[1], 128):
            own = jnp.where(line == at, ref[:, k : k + 128].astype(F32), own)
            at += 1
    message_ref[...] = (spread + own[None]).reshape(ROWS * chips, 128).astype(BF)


def place_kernel(plane, chips, item_rows, ids_ref, pick_ref, chosen_ref):
    ids = ids_ref[...]
    first = jnp.zeros(ids.shape, F32)
    last = jnp.zeros(ids.shape, F32)
    for which in range(2):
        key, low, high, _ = asked_keys(which, plane, chips, item_rows, ids)
        first = first + jnp.sum(jnp.where(low == key, 1.0, 0.0), axis=0, keepdims=True)
        last = last + jnp.sum(jnp.where(high == key, 1.0, 0.0), axis=0, keepdims=True)
    place = jnp.where(first > 0.0, 0, jnp.where(last > 0.0, 2, 1))
    holder = lax.shift_right_logical(ids, item_rows.bit_length() - 1)
    pick_ref[...] = (((holder // plane) & 1) ^ lax.axis_index("core")) * CAP + place
    chip_of = (holder // (2 * plane)) * plane + holder % plane
    chip = lax.broadcasted_iota(jnp.int32, chosen_ref.shape, 0)
    chosen_ref[...] = jnp.where(chip == chip_of, 1.0, 0.0).astype(BF)


def hold_kernel(
    asked_ref, own_ref, other_ref, w_first_ref, w_second_ref, w_score_ref, out_ref, logits_ref
):
    contexts = asked_ref.shape[0]
    tables = (own_ref, other_ref)
    item_rows, width = own_ref.shape
    feature_width = w_first_ref.shape[0] - width
    query = asked_ref[:, :width]
    lane = lax.broadcasted_iota(jnp.int32, (contexts, 128), 1)
    chunk = 512
    peak = jnp.full((contexts, 128), -1e30, F32)
    for core in range(2):
        for start in range(0, item_rows, chunk):
            logits = dot_nt(query, tables[core][start : start + chunk, :])
            at = core * item_rows + start
            logits_ref[:, at : at + chunk] = logits
            for k in range(0, chunk, 128):
                peak = jnp.maximum(peak, logits[:, k : k + 128])
    peak = jnp.max(peak, axis=1, keepdims=True)
    total = jnp.zeros((contexts, 128), F32)
    for start in range(0, 2 * item_rows, 128):
        total = total + jnp.exp(logits_ref[:, start : start + 128] - peak)
    total = jnp.sum(total, axis=1, keepdims=True)
    out = jnp.where(lane == 4 * CAP, peak, jnp.where(lane == 4 * CAP + 1, total, 0.0))

    context_part = dot_nn(
        asked_ref[:, width : width + feature_width], w_first_ref[:feature_width, :]
    )
    query_wide = query.astype(F32)
    id_parts = asked_ref[:, width + feature_width :].astype(F32)
    item = lax.broadcasted_iota(jnp.int32, (contexts, item_rows), 1)
    w_score = jnp.broadcast_to(w_score_ref[...], (128, w_score_ref.shape[1]))
    for core in range(2):
        for j in range(CAP):
            place = core * CAP + j
            inside = id_parts[:, 2 * place : 2 * place + 1] * 256.0
            inside = (inside + id_parts[:, 2 * place + 1 : 2 * place + 2]).astype(jnp.int32)
            chosen = jnp.where(item == inside, 1.0, 0.0).astype(BF)
            rows = dot_nn(chosen, tables[core][...])
            gen = jnp.sum(rows * query_wide, axis=1, keepdims=True)
            hidden = silu(dot_nn(rows.astype(BF), w_first_ref[feature_width:, :]) + context_part)
            second = silu(dot_nn(hidden.astype(BF), w_second_ref[...]))
            score = dot_nt(second.astype(BF), w_score)
            out = jnp.where(lane == place, score, out)
            out = jnp.where(lane == 2 * CAP + place, gen, out)
    out_ref[...] = out


def own_kernel(
    total_items,
    back_ref, chosen_ref, pick_ref, length_ref, logged_ref, prop_ref, section_ref, weight_ref,
):
    slots = pick_ref.shape[1]
    back = jnp.transpose(back_ref[...])[:16]
    peaks, sums = back[4 * CAP : 4 * CAP + 1], back[4 * CAP + 1 : 4 * CAP + 2]
    peak = jnp.max(peaks, axis=1, keepdims=True)
    log_norm = peak + jnp.log(jnp.sum(sums * jnp.exp(peaks - peak), axis=1, keepdims=True))
    chosen = chosen_ref[...]
    top = back.astype(BF)
    rest = back - top.astype(F32)
    middle = rest.astype(BF)
    low = (rest - middle.astype(F32)).astype(BF)
    found = dot_nn(top, chosen) + dot_nn(middle, chosen) + dot_nn(low, chosen)
    pick = pick_ref[...]
    score = jnp.zeros((1, slots), F32)
    gen = jnp.zeros((1, slots), F32)
    for place in range(2 * CAP):
        score = jnp.where(pick == place, found[place : place + 1], score)
        gen = jnp.where(pick == place, found[2 * CAP + place : 2 * CAP + place + 1], gen)
    slot = lax.broadcasted_iota(jnp.int32, (1, slots), 1)
    length = length_ref[0]
    live = slot < length
    masked = jnp.where(live, score, -1e30)
    rank_peak = jnp.max(masked, axis=1, keepdims=True)
    rank_sum = jnp.sum(jnp.where(live, jnp.exp(masked - rank_peak), 0.0), axis=1, keepdims=True)
    rank_norm = rank_peak + jnp.log(rank_sum)
    section = jnp.where(live, score - rank_norm + gen - log_norm + math.log(total_items), 0.0)
    section_ref[...] = section
    chosen = jnp.sum(jnp.where(slot == logged_ref[0], section, 0.0), axis=1, keepdims=True)
    ones = jnp.ones((1, 128), F32)
    weight_ref[...] = (
        chosen
        + jnp.log(ones * length.astype(F32))
        - jnp.log(ones * (prop_ref[0].astype(F32) / 1024.0))
    )


def body(
    query, item_table, context_features, candidates, lengths, logged_slot, logging_prop,
    w_first, w_second, w_score,
):
    item_rows, width = item_table.shape
    slots = candidates.shape[1]
    chips = lax.axis_size(CHIPS)
    plane = lax.axis_size(("x", "z"))
    vmem = pl.BlockSpec(memory_space=pltpu.VMEM)
    smem = pl.BlockSpec(memory_space=pltpu.SMEM)

    other_table = lax.ppermute(item_table, "core", [(0, 1), (1, 0)])
    message = pl.pallas_call(
        lambda *refs: ask_kernel(plane, chips, item_rows, *refs),
        out_shape=jax.ShapeDtypeStruct((ROWS * chips, 128), BF),
        in_specs=[vmem] * 3,
        out_specs=vmem,
        name="ask",
    )(query, context_features, candidates)
    asked = lax.all_to_all(
        message.reshape(chips, ROWS, 128), CHIPS, split_axis=0, concat_axis=0, tiled=True
    ).reshape(chips, ROWS * 128)
    pick, chosen = pl.pallas_call(
        lambda *refs: place_kernel(plane, chips, item_rows, *refs),
        out_shape=(
            jax.ShapeDtypeStruct((1, slots), jnp.int32),
            jax.ShapeDtypeStruct((chips, slots), BF),
        ),
        in_specs=[vmem],
        out_specs=(vmem, vmem),
        cost_estimate=pl.CostEstimate(flops=4000000, bytes_accessed=600000, transcendentals=0),
        name="place",
    )(candidates)
    answers = pl.pallas_call(
        hold_kernel,
        out_shape=jax.ShapeDtypeStruct((chips, 128), F32),
        in_specs=[vmem] * 6,
        out_specs=vmem,
        scratch_shapes=[pltpu.VMEM((chips, 2 * item_rows), F32)],
        compiler_params=pltpu.CompilerParams(vmem_limit_bytes=40 * 1024 * 1024),
        name="hold",
    )(asked, item_table, other_table, w_first, w_second, w_score.reshape(1, -1))
    back = lax.all_to_all(
        answers.reshape(chips, 1, 128), CHIPS, split_axis=0, concat_axis=0, tiled=True
    ).reshape(chips, 128)
    total_items = item_rows * 2 * chips
    section, weight = pl.pallas_call(
        lambda *refs: own_kernel(total_items, *refs),
        out_shape=(
            jax.ShapeDtypeStruct((1, slots), F32),
            jax.ShapeDtypeStruct((1, 128), F32),
        ),
        in_specs=[vmem] * 3 + [smem] * 3,
        out_specs=(vmem, vmem),
        name="own",
    )(back, chosen, pick, lengths, logged_slot, logging_prop)
    return section, weight[0, :1]


def solution(mesh):
    split = Mesh(mesh.devices.reshape(8, 2, 4, 8), ALL)
    row, flat = P(ALL, None), P(ALL)
    placed = (row, row, row, row, flat, flat, flat, P(), P(), P())
    return jax.shard_map(
        body, mesh=split, in_specs=placed, out_specs=(row, flat), check_vma=False
    )
```

time: 96 us -> 81.7 us (0.85)
  between operations: 16.1 us -> 2.68 us
  starting transfers between devices: 33 us -> 36.3 us
  local copies, waits for them, and re-layouts: 4.29 us -> 1.8 us
  waiting for transfers between devices: 29.6 us -> 27.2 us
  Pallas kernels: 11.9 us -> 13.3 us
    ppermute x0 -> x1, starting transfers between devices: none -> 8.79 us  [body(): other_table = lax.ppermute(item_table, 'core', [(0, 1), (1, 0)])]
    all_to_all x1, starting transfers between devices: 23.4 us -> 18.2 us  [body(): lax.all_to_all(message.reshape(chips, ROWS, 128), CHIPS, split_axis=0, co...]
    pallas_call x1 -> x2, Pallas kernels: 2.16 us -> 4.67 us  [the longest x1 2.45 us: body(): pl.pallas_call(lambda *refs: place_kernel(plane, chips, item_rows, *refs)...]
    unnamed x12 -> x11, local copies, waits for them, and re-layouts: 4.29 us -> 1.8 us
    all_to_all x1, waiting for transfers between devices: 10.2 us -> 7.84 us  [body(): lax.all_to_all(answers.reshape(chips, 1, 128), CHIPS, split_axis=0, conca...]
    pallas_call x1, Pallas kernels: 3.8 us -> 2.7 us  [body(): pl.pallas_call(lambda *refs: ask_kernel(plane, chips, item_rows, *refs),...]
  transfers between devices with their start and end apart: 3 -> 3, of which waited for: 2 -> 2; matrix products, arithmetic and copies ran while one was open for 2% -> 1% of each run, Pallas kernels for 4% -> 6%
where the time goes in v2:
time: 81.7 us; the launch traced here: 81.3 us
  starting transfers between devices  36.3 us (44%)
  waiting for transfers between devices  27.2 us (33%)
  Pallas kernels  13.3 us (16%)
  between operations  2.68 us (3%)
  local copies, waits for them, and re-layouts  1.8 us (2%)
    all_to_all x1, waiting for transfers between devices, body(): lax.all_to_all(message.reshape(chips, ROWS, 128), CHIPS, split_axis=0, co...  19.3 us
    all_to_all x1, starting transfers between devices, body(): lax.all_to_all(message.reshape(chips, ROWS, 128), CHIPS, split_axis=0, co...  18.2 us
    all_to_all x1, starting transfers between devices, body(): lax.all_to_all(answers.reshape(chips, 1, 128), CHIPS, split_axis=0, conca...  9.31 us
    ppermute x1, starting transfers between devices, body(): other_table = lax.ppermute(item_table, 'core', [(0, 1), (1, 0)])  8.79 us
    all_to_all x1, waiting for transfers between devices, body(): lax.all_to_all(answers.reshape(chips, 1, 128), CHIPS, split_axis=0, conca...  7.84 us
    pallas_call x1, Pallas kernels, body(): pl.pallas_call(hold_kernel, out_shape=jax.ShapeDtypeStruct((chips, 128),...  5.95 us
    pallas_call x1, Pallas kernels, body(): pl.pallas_call(lambda *refs: ask_kernel(plane, chips, item_rows, *refs),...  2.7 us
    pallas_call x1, Pallas kernels, body(): pl.pallas_call(lambda *refs: place_kernel(plane, chips, item_rows, *refs)...  2.45 us
  transfers between devices with their start and end apart: 3, of which 2 were waited for; matrix products, arithmetic and copies ran while one was open for 1% of the time, Pallas kernels for 6%

profile of v2, /device:TPU:1, one launch (start us, length us, event | category | flops | bytes accessed | tf_op | source)
XLA Modules:
  0.0 81.3 jit_solution(1104382537160939605)
XLA Ops:
  0.6 8.8 %collective-permute-start = (bf16[2048,256]{1,0:T(8,128)(2,1)}, bf16[2048,256]{1,0:T(8,128)(2,1)S(1)}, u32[]{:S(2)}, u32[]{:S(2)}) collective-permute-start(bf16[2048,256]{1,0:T(8,128)(2,1)} %own_ref.1), channel_id=1, source_target_pairs={{0,32},{32,0},{1,33},{33,1},{2,34},{34,2},{3,35},{35,3},{4,36},{36... | collective-permute-start | bytes 3145736 | tf_op jit(solution)/shard_map/ppermute | solution.py:192
  9.4 0.0 copy-start.4
  9.4 0.0 copy-start.2
  9.4 2.7 %ask.1 = bf16[2048,128]{1,0:T(8,128)(2,1)} custom-call(bf16[1,256]{1,0:T(2,128)(2,1)} %refs_0_.2, bf16[1,512]{1,0:T(2,128)(2,1)} %refs_1_.1, s32[1,1024]{1,0:T(1,128)} %refs_0_.3), custom_call_target="tpu_custom_call" | custom-call | tf_op jit(solution)/shard_map/ask/pallas_call | solution.py:193
  12.1 0.0 copy-start
  12.1 18.2 %all-to-all-start = ((bf16[256,8,128]{2,1,0:T(8,128)(2,1)}), bf16[256,8,128]{2,1,0:T(8,128)(2,1)}, u32[]{:S(2)}, u32[]{:S(2)}) async-start(bf16[256,8,128]{2,1,0:T(8,128)(2,1)} %bitcast.12), calls=%async_computation | async-start | bytes 1048576 | tf_op jit(solution)/shard_map/all_to_all | solution.py:200
  30.4 0.0 copy-done.4
  30.4 0.0 copy-start.1
  30.4 19.3 %all-to-all-done = bf16[256,8,128]{2,1,0:T(8,128)(2,1)} async-done(((bf16[256,8,128]{2,1,0:T(8,128)(2,1)}), bf16[256,8,128]{2,1,0:T(8,128)(2,1)}, u32[]{:S(2)}, u32[]{:S(2)}) %all-to-all-start) | async-done | bytes 524320 | tf_op jit(solution)/shard_map/all_to_all | solution.py:200
  49.7 1.1 %copy.15 = bf16[32,8,8,128]{3,1,2,0:T(8,128)(2,1)S(1)} copy(bf16[32,8,8,128]{3,2,1,0:T(8,128)(2,1)} %bitcast.6) | data formatting | bytes 1048576
  50.9 0.0 collective-permute-done.other_ref
  50.9 0.0 copy-done.2
  50.9 0.0 copy-done
  50.9 0.0 copy-done.1
  50.9 6.0 %hold.1 = f32[256,128]{1,0:T(8,128)} custom-call(bf16[256,1024]{1,0:T(8,128)(2,1)S(1)} %bitcast.11, bf16[2048,256]{1,0:T(8,128)(2,1)S(1)} %copy-done, bf16[2048,256]{1,0:T(8,128)(2,1)S(1)} %collective-permute-done.other_ref, bf16[768,512]{1,0:T(8,128)(2,1)S(1)} %copy-done.1, bf16[512,512]{1,0:T(8,128)(2,1)S(1)} %copy-done.2, ...), custom_call_target="tpu_custom_call" | custom-call | tf_op jit(solution)/shard_map/hold/pallas_call | solution.py:214
  56.9 9.3 %all-to-all-start.1 = ((f32[256,1,128]{2,1,0:T(1,128)}), f32[256,1,128]{2,1,0:T(1,128)S(1)}, u32[]{:S(2)}, u32[]{:S(2)}) async-start(f32[256,1,128]{2,1,0:T(1,128)} %bitcast.2), calls=%async_computation.1 | async-start | bytes 262144 | tf_op jit(solution)/shard_map/all_to_all | solution.py:223
  68.1 2.5 %place.1 = (s32[1,1024]{1,0:T(1,128)}, bf16[256,1024]{1,0:T(8,128)(2,1)}) custom-call(s32[1,1024]{1,0:T(1,128)} %refs_0_.3), custom_call_target="tpu_custom_call" | custom-call | flops 4000000 | bytes 600000 | tf_op jit(solution)/shard_map/place/pallas_call | solution.py:203
  70.6 7.8 %all-to-all-done.1 = f32[256,1,128]{2,1,0:T(1,128)S(1)} async-done(((f32[256,1,128]{2,1,0:T(1,128)}), f32[256,1,128]{2,1,0:T(1,128)S(1)}, u32[]{:S(2)}, u32[]{:S(2)}) %all-to-all-start.1) | async-done | bytes 131104 | tf_op jit(solution)/shard_map/all_to_all | solution.py:223
  78.4 0.0 copy-start.3
  78.4 0.6 copy-done.3
  79.1 2.2 %own.1 = (f32[1,1024]{1,0:T(1,128)}, f32[1,128]{1,0:T(1,128)}) custom-call(f32[256,128]{1,0:T(8,128)} %bitcast.13, bf16[256,1024]{1,0:T(8,128)(2,1)} %get-tuple-element.6.refs_1_, s32[1,1024]{1,0:T(1,128)} %get-tuple-element.7.refs_2_, s32[1]{0:T(128)S(6)} %copy.16.refs_3_, s32[1]{0:T(128)S(6)} %copy.17.refs_4_, s32[1]{0:T(128)S(6)} %copy.18.refs_5_), custom_call_target="tpu_custom_call" | custom-call | tf_op jit(solution)/shard_map/own/pallas_call | solution.py:227
  (1 shorter events, 0.0 us)
Async XLA Ops:
  0.6 50.2 %collective-permute-start = (bf16[2048,256]{1,0:T(8,128)(2,1)}, bf16[2048,256]{1,0:T(8,128)(2,1)S(1)}, u32[]{:S(2)}, u32[]{:S(2)}) collective-permute-start(bf16[2048,256]{1,0:T(8,128)(2,1)} %own_ref.1), channel_id=1, source_target_pairs={{0,32},{32,0},{1,33},{33,1},{2,34},{34,2},{3,35},{35,3},{4,36},{36... | collective-permute-start | bytes 3145736 | tf_op jit(solution)/shard_map/ppermute | solution.py:192
  9.4 20.9 %copy-start.4 = (bf16[512]{0:T(512)(128)(2,1)S(1)}, bf16[512]{0:T(512)(128)(2,1)}, u32[]{:S(2)}) copy-start(bf16[512]{0:T(512)(128)(2,1)} %param.19) | copy-start | bytes 3076
  9.4 41.5 %copy-start.2 = (bf16[512,512]{1,0:T(8,128)(2,1)S(1)}, bf16[512,512]{1,0:T(8,128)(2,1)}, u32[]{:S(2)}) copy-start(bf16[512,512]{1,0:T(8,128)(2,1)} %w_second_ref.1) | copy-start | bytes 1572868
  12.1 38.8 %copy-start = (bf16[2048,256]{1,0:T(8,128)(2,1)S(1)}, bf16[2048,256]{1,0:T(8,128)(2,1)}, u32[]{:S(2)}) copy-start(bf16[2048,256]{1,0:T(8,128)(2,1)} %own_ref.1) | copy-start | bytes 3145732
  12.1 37.6 %all-to-all-start = ((bf16[256,8,128]{2,1,0:T(8,128)(2,1)}), bf16[256,8,128]{2,1,0:T(8,128)(2,1)}, u32[]{:S(2)}, u32[]{:S(2)}) async-start(bf16[256,8,128]{2,1,0:T(8,128)(2,1)} %bitcast.12), calls=%async_computation | async-start | bytes 1048576 | tf_op jit(solution)/shard_map/all_to_all | solution.py:200
  30.4 20.5 %copy-start.1 = (bf16[768,512]{1,0:T(8,128)(2,1)S(1)}, bf16[768,512]{1,0:T(8,128)(2,1)}, u32[]{:S(2)}) copy-start(bf16[768,512]{1,0:T(8,128)(2,1)} %w_first_ref.1) | copy-start | bytes 2359300
  56.9 21.5 %all-to-all-start.1 = ((f32[256,1,128]{2,1,0:T(1,128)}), f32[256,1,128]{2,1,0:T(1,128)S(1)}, u32[]{:S(2)}, u32[]{:S(2)}) async-start(f32[256,1,128]{2,1,0:T(1,128)} %bitcast.2), calls=%async_computation.1 | async-start | bytes 262144 | tf_op jit(solution)/shard_map/all_to_all | solution.py:223
  78.4 0.6 copy-start.3

commit v3 on v2

v3 whole, which is shorter than its diff:
```python
import math

import jax
import jax.numpy as jnp
from jax import lax
from jax.experimental import pallas as pl
from jax.experimental.pallas import tpu as pltpu
from jax.sharding import Mesh
from jax.sharding import PartitionSpec as P

ALL = ("y", "core", "x", "z")
CHIPS = ("y", "x", "z")
BIG = float(1 << 24)
CAP = 3
ROWS = 8
MIB = 1 << 20
BF = jnp.bfloat16
F32 = jnp.float32


def dot_nt(a, b):
    return lax.dot_general(a, b, (((1,), (1,)), ((), ())), preferred_element_type=F32)


def dot_nn(a, b):
    return lax.dot_general(a, b, (((1,), (0,)), ((), ())), preferred_element_type=F32)


def silu(v):
    half = 0.5 * v
    return half + half * jnp.tanh(half)


def asked_keys(which, plane, chips, item_rows, ids):
    holder = lax.shift_right_logical(ids, item_rows.bit_length() - 1)
    slot = lax.broadcasted_iota(jnp.int32, ids.shape, 1)
    key = (slot * item_rows + (ids & (item_rows - 1))).astype(F32)
    core = lax.axis_index("core") ^ which
    chip = lax.broadcasted_iota(jnp.int32, (chips, 1), 0)
    device = (chip // plane) * (2 * plane) + core * plane + chip % plane
    mine = holder == device
    low = jnp.min(jnp.where(mine, key, BIG), axis=1, keepdims=True)
    high = jnp.max(jnp.where(mine, key, -1.0), axis=1, keepdims=True)
    total = jnp.sum(jnp.where(mine, key, 0.0), axis=1, keepdims=True)
    return key, low, high, total


def ask_kernel(plane, chips, item_rows, query_ref, feature_ref, ids_ref, message_ref, spread_ref):
    ids = ids_ref[...]
    lane = lax.broadcasted_iota(jnp.int32, (chips, 128), 1)
    wanted = jnp.full((chips, 128), -1.0, F32)
    for which in range(2):
        _, low, high, total = asked_keys(which, plane, chips, item_rows, ids)
        middle = total - low - high
        least = jnp.where(high >= 0.0, low, -1.0)
        middle = jnp.where((high > low) & (middle > 0.0), middle, -1.0)
        most = jnp.where(high > low, high, -1.0)
        for j, keys in enumerate((least, middle, most)):
            at = 2 * (which * CAP + j)
            wanted = jnp.where((lane == at) | (lane == at + 1), keys, wanted)
    wanted = wanted.astype(jnp.int32)
    inside = jnp.where(wanted < 0, 2 * item_rows, wanted & (item_rows - 1))
    asked = jnp.where((lane & 1) == 0, lax.shift_right_logical(inside, 8), inside & 255)
    asked = asked.astype(F32)
    spread_ref[pl.ds(ROWS - 2, chips, stride=ROWS), :] = asked
    line = lax.broadcasted_iota(jnp.int32, (ROWS, 128), 0)
    own = jnp.zeros((ROWS, 128), F32)
    at = 0
    for ref in (query_ref, feature_ref):
        for k in range(0, ref.shape[1], 128):
            own = jnp.where(line == at, ref[:, k : k + 128].astype(F32), own)
            at += 1
    spread = spread_ref[...].reshape(chips, ROWS, 128)
    spread = jnp.where((line == ROWS - 2)[None], spread, own[None])
    message_ref[...] = spread.reshape(ROWS * chips, 128).astype(BF)


def place_kernel(
    plane, chips, item_rows, ids_ref, length_ref, logged_ref, prop_ref, facts_ref, chosen_ref
):
    ids = ids_ref[...]
    first = jnp.zeros(ids.shape, F32)
    last = jnp.zeros(ids.shape, F32)
    for which in range(2):
        key, low, high, _ = asked_keys(which, plane, chips, item_rows, ids)
        first = first + jnp.sum(jnp.where(low == key, 1.0, 0.0), axis=0, keepdims=True)
        last = last + jnp.sum(jnp.where(high == key, 1.0, 0.0), axis=0, keepdims=True)
    place = jnp.where(first > 0.0, 0, jnp.where(last > 0.0, 2, 1))
    holder = lax.shift_right_logical(ids, item_rows.bit_length() - 1)
    place = (((holder // plane) & 1) ^ lax.axis_index("core")) * CAP + place
    slot = lax.broadcasted_iota(jnp.int32, ids.shape, 1)
    ones = jnp.ones(ids.shape, F32)
    length = length_ref[0]
    facts_ref[0:1] = place.astype(F32)
    facts_ref[1:2] = jnp.where(slot < length, 1.0, 0.0)
    facts_ref[2:3] = jnp.where(slot == logged_ref[0], 1.0, 0.0)
    facts_ref[3:4] = jnp.log(ones * length.astype(F32)) - jnp.log(
        ones * (prop_ref[0].astype(F32) / 1024.0)
    )
    chip_of = (holder // (2 * plane)) * plane + holder % plane
    chip = lax.broadcasted_iota(jnp.int32, chosen_ref.shape, 0)
    chosen_ref[...] = jnp.where(chip == chip_of, 1.0, 0.0).astype(BF)


def hold_kernel(
    asked_ref, own_ref, other_ref, w_first_ref, w_second_ref, w_score_ref, out_ref, lines_ref
):
    contexts = asked_ref.shape[0] // ROWS
    tables = (own_ref, other_ref)
    item_rows, width = own_ref.shape
    feature_width = w_first_ref.shape[0] - width
    lines_ref[...] = asked_ref[...].astype(F32)
    lines = [lines_ref[pl.ds(k, contexts, stride=ROWS), :] for k in range(ROWS - 1)]
    query_wide = jnp.concatenate(lines[: width // 128], axis=1)
    query = query_wide.astype(BF)
    features = jnp.concatenate(lines[width // 128 : ROWS - 2], axis=1).astype(BF)
    id_parts = lines[ROWS - 2]
    lane = lax.broadcasted_iota(jnp.int32, (contexts, 128), 1)
    chunk = 1024
    peak = jnp.full((contexts, 128), -1e30, F32)
    total = jnp.zeros((contexts, 128), F32)
    for core in range(2):
        for start in range(0, item_rows, chunk):
            logits = dot_nt(query, tables[core][start : start + chunk, :])
            new = peak
            for k in range(0, chunk, 128):
                new = jnp.maximum(new, logits[:, k : k + 128])
            total = total * jnp.exp(peak - new)
            for k in range(0, chunk, 128):
                total = total + jnp.exp(logits[:, k : k + 128] - new)
            peak = new
    top = jnp.max(peak, axis=1, keepdims=True)
    total = jnp.sum(total * jnp.exp(peak - top), axis=1, keepdims=True)
    out = jnp.where(lane == 4 * CAP, top, jnp.where(lane == 4 * CAP + 1, total, 0.0))

    context_part = dot_nn(features, w_first_ref[:feature_width, :])
    item = lax.broadcasted_iota(jnp.int32, (contexts, item_rows), 1)
    w_score = jnp.broadcast_to(w_score_ref[...], (128, w_score_ref.shape[1]))
    for core in range(2):
        for j in range(CAP):
            place = core * CAP + j
            inside = id_parts[:, 2 * place : 2 * place + 1] * 256.0
            inside = (inside + id_parts[:, 2 * place + 1 : 2 * place + 2]).astype(jnp.int32)
            chosen = jnp.where(item == inside, 1.0, 0.0).astype(BF)
            rows = dot_nn(chosen, tables[core][...])
            gen = jnp.sum(rows * query_wide, axis=1, keepdims=True)
            hidden = silu(dot_nn(rows.astype(BF), w_first_ref[feature_width:, :]) + context_part)
            second = silu(dot_nn(hidden.astype(BF), w_second_ref[...]))
            score = dot_nt(second.astype(BF), w_score)
            out = jnp.where(lane == place, score, out)
            out = jnp.where(lane == 2 * CAP + place, gen, out)
    out_ref[...] = out


def own_kernel(total_items, back_ref, chosen_ref, facts_ref, section_ref, weight_ref):
    back = jnp.transpose(back_ref[...])[:16]
    top = back.astype(BF)
    rest = back - top.astype(F32)
    middle = rest.astype(BF)
    low = (rest - middle.astype(F32)).astype(BF)
    found = dot_nn(jnp.concatenate([top, middle, low], axis=0), chosen_ref[...])
    found = found[:16] + found[16:32] + found[32:]
    peaks, sums = back[4 * CAP : 4 * CAP + 1], back[4 * CAP + 1 : 4 * CAP + 2]
    peak = jnp.max(peaks, axis=1, keepdims=True)
    log_norm = peak + jnp.log(jnp.sum(sums * jnp.exp(peaks - peak), axis=1, keepdims=True))
    place = facts_ref[0:1]
    live = facts_ref[1:2] > 0.0
    score = jnp.zeros(place.shape, F32)
    gen = jnp.zeros(place.shape, F32)
    for k in range(2 * CAP):
        score = jnp.where(place == k, found[k : k + 1], score)
        gen = jnp.where(place == k, found[2 * CAP + k : 2 * CAP + k + 1], gen)
    masked = jnp.where(live, score, -1e30)
    rank_peak = jnp.max(masked, axis=1, keepdims=True)
    rank_sum = jnp.sum(jnp.where(live, jnp.exp(masked - rank_peak), 0.0), axis=1, keepdims=True)
    rank_norm = rank_peak + jnp.log(rank_sum)
    section = jnp.where(live, score - rank_norm + gen - log_norm + math.log(total_items), 0.0)
    section_ref[...] = section
    chosen = jnp.sum(jnp.where(facts_ref[2:3] > 0.0, section, 0.0), axis=1, keepdims=True)
    weight_ref[...] = chosen + facts_ref[3:4, :128]


def body(
    query, item_table, context_features, candidates, lengths, logged_slot, logging_prop,
    w_first, w_second, w_score,
):
    item_rows, width = item_table.shape
    slots = candidates.shape[1]
    chips = lax.axis_size(CHIPS)
    plane = lax.axis_size(("x", "z"))
    vmem = pl.BlockSpec(memory_space=pltpu.VMEM)
    smem = pl.BlockSpec(memory_space=pltpu.SMEM)

    message = pl.pallas_call(
        lambda *refs: ask_kernel(plane, chips, item_rows, *refs),
        out_shape=jax.ShapeDtypeStruct((ROWS * chips, 128), BF),
        in_specs=[vmem] * 3,
        out_specs=vmem,
        scratch_shapes=[pltpu.VMEM((ROWS * chips, 128), F32)],
        compiler_params=pltpu.CompilerParams(vmem_limit_bytes=60 * MIB),
        name="ask",
    )(query, context_features, candidates)
    other_table = lax.ppermute(item_table, "core", [(0, 1), (1, 0)])
    asked = lax.all_to_all(
        message.reshape(chips, ROWS, 128), CHIPS, split_axis=0, concat_axis=0, tiled=True
    ).reshape(ROWS * chips, 128)
    facts, chosen = pl.pallas_call(
        lambda *refs: place_kernel(plane, chips, item_rows, *refs),
        out_shape=(
            jax.ShapeDtypeStruct((8, slots), F32),
            jax.ShapeDtypeStruct((chips, slots), BF),
        ),
        in_specs=[vmem] + [smem] * 3,
        out_specs=(vmem, vmem),
        compiler_params=pltpu.CompilerParams(vmem_limit_bytes=8 * MIB),
        cost_estimate=pl.CostEstimate(flops=20000000000, bytes_accessed=600000, transcendentals=0),
        name="place",
    )(candidates, lengths, logged_slot, logging_prop)
    asked, facts = lax.optimization_barrier((asked, facts))
    answers = pl.pallas_call(
        hold_kernel,
        out_shape=jax.ShapeDtypeStruct((chips, 128), F32),
        in_specs=[vmem] * 6,
        out_specs=vmem,
        scratch_shapes=[pltpu.VMEM((ROWS * chips, 128), F32)],
        compiler_params=pltpu.CompilerParams(vmem_limit_bytes=16 * MIB),
        name="hold",
    )(asked, item_table, other_table, w_first, w_second, w_score.reshape(1, -1))
    back = lax.all_to_all(
        answers.reshape(chips, 1, 128), CHIPS, split_axis=0, concat_axis=0, tiled=True
    ).reshape(chips, 128)
    total_items = item_rows * 2 * chips
    section, weight = pl.pallas_call(
        lambda *refs: own_kernel(total_items, *refs),
        out_shape=(
            jax.ShapeDtypeStruct((1, slots), F32),
            jax.ShapeDtypeStruct((1, 128), F32),
        ),
        in_specs=[vmem] * 3,
        out_specs=(vmem, vmem),
        compiler_params=pltpu.CompilerParams(vmem_limit_bytes=8 * MIB),
        name="own",
    )(back, chosen, facts)
    return section, weight[0, :1]


def solution(mesh):
    split = Mesh(mesh.devices.reshape(8, 2, 4, 8), ALL)
    row, flat = P(ALL, None), P(ALL)
    placed = (row, row, row, row, flat, flat, flat, P(), P(), P())
    return jax.shard_map(
        body, mesh=split, in_specs=placed, out_specs=(row, flat), check_vma=False
    )
```

time: 81.7 us -> 75.5 us (0.924)
  blocking collectives: 0 us -> 21.7 us
  waiting for transfers between devices: 27.2 us -> 12.1 us
  starting transfers between devices: 36.3 us -> 26.1 us
  Pallas kernels: 13.3 us -> 9.96 us
    all_to_all x0 -> x1, blocking collectives: none -> 21.7 us  [body(): lax.all_to_all(answers.reshape(chips, 1, 128), CHIPS, split_axis=0, conca...]
    all_to_all x1 -> x0, starting transfers between devices: 9.31 us -> none  [body(): lax.all_to_all(answers.reshape(chips, 1, 128), CHIPS, split_axis=0, conca...]
    all_to_all x1 -> x0, waiting for transfers between devices: 7.84 us -> none  [body(): lax.all_to_all(answers.reshape(chips, 1, 128), CHIPS, split_axis=0, conca...]
    all_to_all x1, waiting for transfers between devices: 19.3 us -> 12.1 us  [body(): lax.all_to_all(message.reshape(chips, ROWS, 128), CHIPS, split_axis=0, co...]
    ppermute x1, starting transfers between devices: 8.79 us -> 2.86 us  [body(): other_table = lax.ppermute(item_table, 'core', [(0, 1), (1, 0)])]
    all_to_all x1, starting transfers between devices: 18.2 us -> 23.2 us  [body(): lax.all_to_all(message.reshape(chips, ROWS, 128), CHIPS, split_axis=0, co...]
    pallas_call x1, Pallas kernels: 2.45 us -> 1.09 us  [body(): pl.pallas_call(lambda *refs: place_kernel(plane, chips, item_rows, *refs)...]
    pallas_call x1, Pallas kernels: 2.22 us -> 1.04 us  [body(): pl.pallas_call(lambda *refs: own_kernel(total_items, *refs), out_shape=(j...]
  transfers between devices with their start and end apart: 3 -> 2, of which waited for: 2 -> 1; matrix products, arithmetic and copies ran while one was open for 1% -> 0% of each run, Pallas kernels for 6% -> 1%
where the time goes in v3:
time: 75.5 us; the launch traced here: 74.3 us
  starting transfers between devices  26.1 us (35%)
  blocking collectives  21.7 us (29%)
  waiting for transfers between devices  12.1 us (16%)
  Pallas kernels  9.96 us (13%)
  between operations  2.68 us (4%)
  local copies, waits for them, and re-layouts  1.85 us (2%)
    all_to_all x1, starting transfers between devices, body(): lax.all_to_all(message.reshape(chips, ROWS, 128), CHIPS, split_axis=0, co...  23.2 us
    all_to_all x1, blocking collectives, body(): lax.all_to_all(answers.reshape(chips, 1, 128), CHIPS, split_axis=0, conca...  21.7 us
    all_to_all x1, waiting for transfers between devices, body(): lax.all_to_all(message.reshape(chips, ROWS, 128), CHIPS, split_axis=0, co...  12.1 us
    pallas_call x1, Pallas kernels, body(): pl.pallas_call(hold_kernel, out_shape=jax.ShapeDtypeStruct((chips, 128),...  5.39 us
    ppermute x1, starting transfers between devices, body(): other_table = lax.ppermute(item_table, 'core', [(0, 1), (1, 0)])  2.86 us
    pallas_call x1, Pallas kernels, body(): pl.pallas_call(lambda *refs: ask_kernel(plane, chips, item_rows, *refs),...  2.45 us
    unnamed x14, local copies, waits for them, and re-layouts  1.85 us
  transfers between devices with their start and end apart: 2, of which 1 were waited for; matrix products, arithmetic and copies ran while one was open for 0% of the time, Pallas kernels for 1%

profile of v3, /device:TPU:1, one launch (start us, length us, event | category | flops | bytes accessed | tf_op | source)
XLA Modules:
  0.0 74.3 jit_solution(7587296095264961710)
XLA Ops:
  0.6 0.0 copy-start
  0.6 2.4 %ask.1 = bf16[2048,128]{1,0:T(8,128)(2,1)} custom-call(bf16[1,256]{1,0:T(2,128)(2,1)} %refs_0_.2, bf16[1,512]{1,0:T(2,128)(2,1)} %refs_1_.2, s32[1,1024]{1,0:T(1,128)} %refs_0_.3), custom_call_target="tpu_custom_call" | custom-call | tf_op jit(solution)/shard_map/ask/pallas_call | solution.py:194
  3.1 23.2 %all-to-all-start = ((bf16[256,8,128]{2,1,0:T(8,128)(2,1)}), bf16[256,8,128]{2,1,0:T(8,128)(2,1)S(1)}, u32[]{:S(2)}, u32[]{:S(2)}) async-start(bf16[256,8,128]{2,1,0:T(8,128)(2,1)} %bitcast.11), calls=%async_computation | async-start | bytes 1048576 | tf_op jit(solution)/shard_map/all_to_all | solution.py:204
  26.3 0.0 copy-done
  26.3 0.0 copy-start.5
  26.3 2.9 %collective-permute-start = (bf16[2048,256]{1,0:T(8,128)(2,1)S(1)}, bf16[2048,256]{1,0:T(8,128)(2,1)S(1)}, u32[]{:S(2)}, u32[]{:S(2)}) collective-permute-start(bf16[2048,256]{1,0:T(8,128)(2,1)S(1)} %copy-done), channel_id=1, source_target_pairs={{0,32},{32,0},{1,33},{33,1},{2,34},{34,2},{3,35},{35,3},{4,36},{36... | collective-permute-start | bytes 3145736 | tf_op jit(solution)/shard_map/ppermute | solution.py:203
  30.5 0.0 copy-start.6
  31.2 0.0 copy-done.6
  31.2 0.0 copy-done.5
  31.2 0.0 copy-start.1
  31.2 1.1 %place.1 = (f32[8,1024]{1,0:T(8,128)S(1)}, bf16[256,1024]{1,0:T(8,128)(2,1)S(1)}) custom-call(s32[1,1024]{1,0:T(1,128)S(1)} %copy-done.5, s32[1]{0:T(128)S(6)} %copy.13.refs_1_, s32[1]{0:T(128)S(6)} %copy.14.refs_2_, s32[1]{0:T(128)S(6)} %copy.15.refs_3_), custom_call_target="tpu_custom_call" | custom-call | flops 20000000000 | bytes 600000 | tf_op jit(solution)/shard_map/place/pallas_call | solution.py:207
  32.3 0.0 copy-start.3
  32.3 0.8 %copy-done.3 = bf16[256,1024]{1,0:T(8,128)(2,1)} copy-done((bf16[256,1024]{1,0:T(8,128)(2,1)}, bf16[256,1024]{1,0:T(8,128)(2,1)S(1)}, u32[]{:S(2)}) %copy-start.3) | copy-done | bytes 524312
  33.1 12.1 %all-to-all-done = bf16[256,8,128]{2,1,0:T(8,128)(2,1)S(1)} async-done(((bf16[256,8,128]{2,1,0:T(8,128)(2,1)}), bf16[256,8,128]{2,1,0:T(8,128)(2,1)S(1)}, u32[]{:S(2)}, u32[]{:S(2)}) %all-to-all-start) | async-done | bytes 524320 | tf_op jit(solution)/shard_map/all_to_all | solution.py:204
  45.2 0.0 collective-permute-done.other_ref
  45.2 0.0 copy-done.1
  45.2 0.0 copy-start.2
  45.2 1.0 %copy-done.2 = bf16[512,512]{1,0:T(8,128)(2,1)S(1)} copy-done((bf16[512,512]{1,0:T(8,128)(2,1)S(1)}, bf16[512,512]{1,0:T(8,128)(2,1)}, u32[]{:S(2)}) %copy-start.2) | copy-done | bytes 524312
  46.2 0.0 copy-start.4
  46.2 5.4 %hold.1 = f32[256,128]{1,0:T(8,128)S(1)} custom-call(bf16[2048,128]{1,0:T(8,128)(2,1)S(1)} %bitcast.8, bf16[2048,256]{1,0:T(8,128)(2,1)S(1)} %copy-done, bf16[2048,256]{1,0:T(8,128)(2,1)S(1)} %collective-permute-done.other_ref, bf16[768,512]{1,0:T(8,128)(2,1)S(1)} %copy-done.1, bf16[512,512]{1,0:T(8,128)(2,1)S(1)} %copy-done.2, ...), custom_call_target="tpu_custom_call" | custom-call | tf_op jit(solution)/shard_map/hold/pallas_call | solution.py:220
  51.6 21.7 %all_to_all.10 = f32[256,1,128]{2,1,0:T(1,128)S(1)} all-to-all(f32[256,1,128]{2,1,0:T(1,128)S(1)} %bitcast.9), channel_id=1, replica_groups=mesh['y'=8,'core'=2,'x'=4,'z'=8] {'y','x','z'}, dimensions={0} | all-to-all | bytes 262144 | tf_op jit(solution)/shard_map/all_to_all | solution.py:229
  73.3 0.0 copy-done.4
  73.3 1.0 %own.1 = (f32[1,1024]{1,0:T(1,128)}, f32[1,128]{1,0:T(1,128)}) custom-call(f32[256,128]{1,0:T(8,128)S(1)} %bitcast.10, bf16[256,1024]{1,0:T(8,128)(2,1)S(1)} %copy-done.4, f32[8,1024]{1,0:T(8,128)S(1)} %get-tuple-element.11.refs_2_), custom_call_target="tpu_custom_call" | custom-call | tf_op jit(solution)/shard_map/own/pallas_call | solution.py:233
  (1 shorter events, 0.0 us)
Async XLA Ops:
  0.6 25.7 %copy-start = (bf16[2048,256]{1,0:T(8,128)(2,1)S(1)}, bf16[2048,256]{1,0:T(8,128)(2,1)}, u32[]{:S(2)}) copy-start(bf16[2048,256]{1,0:T(8,128)(2,1)} %own_ref.1) | copy-start | bytes 3145732
  3.1 42.1 %all-to-all-start = ((bf16[256,8,128]{2,1,0:T(8,128)(2,1)}), bf16[256,8,128]{2,1,0:T(8,128)(2,1)S(1)}, u32[]{:S(2)}, u32[]{:S(2)}) async-start(bf16[256,8,128]{2,1,0:T(8,128)(2,1)} %bitcast.11), calls=%async_computation | async-start | bytes 1048576 | tf_op jit(solution)/shard_map/all_to_all | solution.py:204
  26.3 4.9 %copy-start.5 = (s32[1,1024]{1,0:T(1,128)S(1)}, s32[1,1024]{1,0:T(1,128)}, u32[]{:S(2)}) copy-start(s32[1,1024]{1,0:T(1,128)} %refs_0_.3) | copy-start | bytes 12292
  26.3 18.8 %collective-permute-start = (bf16[2048,256]{1,0:T(8,128)(2,1)S(1)}, bf16[2048,256]{1,0:T(8,128)(2,1)S(1)}, u32[]{:S(2)}, u32[]{:S(2)}) collective-permute-start(bf16[2048,256]{1,0:T(8,128)(2,1)S(1)} %copy-done), channel_id=1, source_target_pairs={{0,32},{32,0},{1,33},{33,1},{2,34},{34,2},{3,35},{35,3},{4,36},{36... | collective-permute-start | bytes 3145736 | tf_op jit(solution)/shard_map/ppermute | solution.py:203
  30.5 0.7 copy-start.6
  31.2 14.0 %copy-start.1 = (bf16[768,512]{1,0:T(8,128)(2,1)S(1)}, bf16[768,512]{1,0:T(8,128)(2,1)}, u32[]{:S(2)}) copy-start(bf16[768,512]{1,0:T(8,128)(2,1)} %w_first_ref.1) | copy-start | bytes 2359300
  32.3 0.8 %copy-start.3 = (bf16[256,1024]{1,0:T(8,128)(2,1)}, bf16[256,1024]{1,0:T(8,128)(2,1)S(1)}, u32[]{:S(2)}) copy-start(bf16[256,1024]{1,0:T(8,128)(2,1)S(1)} %get-tuple-element.10.refs_1_) | copy-start | bytes 1572868
  45.2 1.0 %copy-start.2 = (bf16[512,512]{1,0:T(8,128)(2,1)S(1)}, bf16[512,512]{1,0:T(8,128)(2,1)}, u32[]{:S(2)}) copy-start(bf16[512,512]{1,0:T(8,128)(2,1)} %w_second_ref.1) | copy-start | bytes 1572868
  46.2 27.1 %copy-start.4 = (bf16[256,1024]{1,0:T(8,128)(2,1)S(1)}, bf16[256,1024]{1,0:T(8,128)(2,1)}, u32[]{:S(2)}) copy-start(bf16[256,1024]{1,0:T(8,128)(2,1)} %copy-done.3) | copy-start | bytes 1572868

commit v4 on v3

--- a/solution.py
+++ b/solution.py
@@ -103,8 +103,11 @@
 
 
 def hold_kernel(
-    asked_ref, own_ref, other_ref, w_first_ref, w_second_ref, w_score_ref, out_ref, lines_ref
+    asked_ref, own_ref, other_hbm, w_first_ref, w_second_ref, w_score_ref,
+    out_ref, lines_ref, other_ref, other_sem,
 ):
+    other_copy = pltpu.make_async_copy(other_hbm, other_ref, other_sem)
+    other_copy.start()
     contexts = asked_ref.shape[0] // ROWS
     tables = (own_ref, other_ref)
     item_rows, width = own_ref.shape
@@ -119,7 +122,13 @@
     chunk = 1024
     peak = jnp.full((contexts, 128), -1e30, F32)
     total = jnp.zeros((contexts, 128), F32)
+    out = jnp.zeros((contexts, 128), F32)
+    context_part = dot_nn(features, w_first_ref[:feature_width, :])
+    item = lax.broadcasted_iota(jnp.int32, (contexts, item_rows), 1)
+    w_score = jnp.broadcast_to(w_score_ref[...], (128, w_score_ref.shape[1]))
     for core in range(2):
+        if core == 1:
+            other_copy.wait()
         for start in range(0, item_rows, chunk):
             logits = dot_nt(query, tables[core][start : start + chunk, :])
             new = peak
@@ -129,14 +138,6 @@
             for k in range(0, chunk, 128):
                 total = total + jnp.exp(logits[:, k : k + 128] - new)
             peak = new
-    top = jnp.max(peak, axis=1, keepdims=True)
-    total = jnp.sum(total * jnp.exp(peak - top), axis=1, keepdims=True)
-    out = jnp.where(lane == 4 * CAP, top, jnp.where(lane == 4 * CAP + 1, total, 0.0))
-
-    context_part = dot_nn(features, w_first_ref[:feature_width, :])
-    item = lax.broadcasted_iota(jnp.int32, (contexts, item_rows), 1)
-    w_score = jnp.broadcast_to(w_score_ref[...], (128, w_score_ref.shape[1]))
-    for core in range(2):
         for j in range(CAP):
             place = core * CAP + j
             inside = id_parts[:, 2 * place : 2 * place + 1] * 256.0
@@ -149,6 +150,9 @@
             score = dot_nt(second.astype(BF), w_score)
             out = jnp.where(lane == place, score, out)
             out = jnp.where(lane == 2 * CAP + place, gen, out)
+    top = jnp.max(peak, axis=1, keepdims=True)
+    total = jnp.sum(total * jnp.exp(peak - top), axis=1, keepdims=True)
+    out = jnp.where(lane == 4 * CAP, top, jnp.where(lane == 4 * CAP + 1, total, out))
     out_ref[...] = out
 
 
@@ -220,10 +224,14 @@
     answers = pl.pallas_call(
         hold_kernel,
         out_shape=jax.ShapeDtypeStruct((chips, 128), F32),
-        in_specs=[vmem] * 6,
+        in_specs=[vmem, vmem, pl.BlockSpec(memory_space=pl.ANY), vmem, vmem, vmem],
         out_specs=vmem,
-        scratch_shapes=[pltpu.VMEM((ROWS * chips, 128), F32)],
-        compiler_params=pltpu.CompilerParams(vmem_limit_bytes=16 * MIB),
+        scratch_shapes=[
+            pltpu.VMEM((ROWS * chips, 128), F32),
+            pltpu.VMEM(item_table.shape, BF),
+            pltpu.SemaphoreType.DMA,
+        ],
+        compiler_params=pltpu.CompilerParams(vmem_limit_bytes=51 * MIB),
         name="hold",
     )(asked, item_table, other_table, w_first, w_second, w_score.reshape(1, -1))
     back = lax.all_to_all(

time: 75.5 us -> 75.1 us (level)
  local copies, waits for them, and re-layouts: 1.85 us -> 0.04 us
  waiting for transfers between devices: 12.1 us -> 12.9 us
    unnamed x14 -> x10, local copies, waits for them, and re-layouts: 1.85 us -> 0.04 us
    all_to_all x1, waiting for transfers between devices: 12.1 us -> 12.9 us  [body(): lax.all_to_all(message.reshape(chips, ROWS, 128), CHIPS, split_axis=0, co...]
where the time goes in v4:
time: 75.1 us; the launch traced here: 74 us
  starting transfers between devices  26.1 us (35%)
  blocking collectives  21.7 us (29%)
  waiting for transfers between devices  12.9 us (17%)
  Pallas kernels  10.7 us (14%)
  between operations  2.68 us (4%)
    all_to_all x1, starting transfers between devices, body(): lax.all_to_all(message.reshape(chips, ROWS, 128), CHIPS, split_axis=0, co...  23.2 us
    all_to_all x1, blocking collectives, body(): lax.all_to_all(answers.reshape(chips, 1, 128), CHIPS, split_axis=0, conca...  21.7 us
    all_to_all x1, waiting for transfers between devices, body(): lax.all_to_all(message.reshape(chips, ROWS, 128), CHIPS, split_axis=0, co...  12.9 us
    pallas_call x1, Pallas kernels, body(): pl.pallas_call(hold_kernel, out_shape=jax.ShapeDtypeStruct((chips, 128),...  6.06 us
    ppermute x1, starting transfers between devices, body(): other_table = lax.ppermute(item_table, 'core', [(0, 1), (1, 0)])  2.86 us
    pallas_call x1, Pallas kernels, body(): pl.pallas_call(lambda *refs: ask_kernel(plane, chips, item_rows, *refs),...  2.48 us
  transfers between devices with their start and end apart: 2, of which 1 were waited for; matrix products, arithmetic and copies ran while one was open for 0% of the time, Pallas kernels for 1%

profile of v4, /device:TPU:1, one launch (start us, length us, event | category | flops | bytes accessed | tf_op | source)
XLA Modules:
  0.0 74.0 jit_solution(3651688813432797517)
XLA Ops:
  0.6 0.0 copy-start
  0.6 2.5 %ask.1 = bf16[2048,128]{1,0:T(8,128)(2,1)} custom-call(bf16[1,256]{1,0:T(2,128)(2,1)} %refs_0_.2, bf16[1,512]{1,0:T(2,128)(2,1)} %refs_1_.2, s32[1,1024]{1,0:T(1,128)} %refs_0_.3), custom_call_target="tpu_custom_call" | custom-call | tf_op jit(solution)/shard_map/ask/pallas_call | solution.py:198
  3.1 23.2 %all-to-all-start = ((bf16[256,8,128]{2,1,0:T(8,128)(2,1)}), bf16[256,8,128]{2,1,0:T(8,128)(2,1)S(1)}, u32[]{:S(2)}, u32[]{:S(2)}) async-start(bf16[256,8,128]{2,1,0:T(8,128)(2,1)} %bitcast.11), calls=%async_computation | async-start | bytes 1048576 | tf_op jit(solution)/shard_map/all_to_all | solution.py:208
  26.3 0.0 copy-done
  26.3 0.0 copy-start.3
  26.3 2.9 %collective-permute-start = (bf16[2048,256]{1,0:T(8,128)(2,1)S(1)}, bf16[2048,256]{1,0:T(8,128)(2,1)}, u32[]{:S(2)}, u32[]{:S(2)}) collective-permute-start(bf16[2048,256]{1,0:T(8,128)(2,1)S(1)} %copy-done), channel_id=1, source_target_pairs={{0,32},{32,0},{1,33},{33,1},{2,34},{34,2},{3,35},{35,3},{4,36},{36... | collective-permute-start | bytes 3145736 | tf_op jit(solution)/shard_map/ppermute | solution.py:207
  30.5 0.0 copy-start.4
  31.2 0.0 copy-done.4
  31.2 0.0 copy-done.3
  31.2 0.0 copy-start.1
  31.2 0.0 copy-start.2
  31.2 1.1 %place.1 = (f32[8,1024]{1,0:T(8,128)S(1)}, bf16[256,1024]{1,0:T(8,128)(2,1)S(1)}) custom-call(s32[1,1024]{1,0:T(1,128)S(1)} %copy-done.3, s32[1]{0:T(128)S(6)} %copy.13.refs_1_, s32[1]{0:T(128)S(6)} %copy.14.refs_2_, s32[1]{0:T(128)S(6)} %copy.15.refs_3_), custom_call_target="tpu_custom_call" | custom-call | flops 20000000000 | bytes 600000 | tf_op jit(solution)/shard_map/place/pallas_call | solution.py:211
  32.3 12.9 %all-to-all-done = bf16[256,8,128]{2,1,0:T(8,128)(2,1)S(1)} async-done(((bf16[256,8,128]{2,1,0:T(8,128)(2,1)}), bf16[256,8,128]{2,1,0:T(8,128)(2,1)S(1)}, u32[]{:S(2)}, u32[]{:S(2)}) %all-to-all-start) | async-done | bytes 524320 | tf_op jit(solution)/shard_map/all_to_all | solution.py:208
  45.2 0.0 collective-permute-done.other_hbm
  45.2 0.0 copy-done.1
  45.2 0.0 copy-done.2
  45.2 6.1 %hold.1 = f32[256,128]{1,0:T(8,128)S(1)} custom-call(bf16[2048,128]{1,0:T(8,128)(2,1)S(1)} %bitcast.8, bf16[2048,256]{1,0:T(8,128)(2,1)S(1)} %copy-done, bf16[2048,256]{1,0:T(8,128)(2,1)} %collective-permute-done.other_hbm, bf16[768,512]{1,0:T(8,128)(2,1)S(1)} %copy-done.1, bf16[512,512]{1,0:T(8,128)(2,1)S(1)} %copy-done.2, ...), custom_call_target="tpu_custom_call" | custom-call | tf_op jit(solution)/shard_map/hold/pallas_call | solution.py:224
  51.3 21.7 %all_to_all.10 = f32[256,1,128]{2,1,0:T(1,128)S(1)} all-to-all(f32[256,1,128]{2,1,0:T(1,128)S(1)} %bitcast.9), channel_id=1, replica_groups=mesh['y'=8,'core'=2,'x'=4,'z'=8] {'y','x','z'}, dimensions={0} | all-to-all | bytes 262144 | tf_op jit(solution)/shard_map/all_to_all | solution.py:237
  73.0 1.0 %own.1 = (f32[1,1024]{1,0:T(1,128)}, f32[1,128]{1,0:T(1,128)}) custom-call(f32[256,128]{1,0:T(8,128)S(1)} %bitcast.10, bf16[256,1024]{1,0:T(8,128)(2,1)S(1)} %get-tuple-element.10.refs_1_, f32[8,1024]{1,0:T(8,128)S(1)} %get-tuple-element.11.refs_2_), custom_call_target="tpu_custom_call" | custom-call | tf_op jit(solution)/shard_map/own/pallas_call | solution.py:241
  (1 shorter events, 0.0 us)
Async XLA Ops:
  0.6 25.7 %copy-start = (bf16[2048,256]{1,0:T(8,128)(2,1)S(1)}, bf16[2048,256]{1,0:T(8,128)(2,1)}, u32[]{:S(2)}) copy-start(bf16[2048,256]{1,0:T(8,128)(2,1)} %own_ref.1) | copy-start | bytes 3145732
  3.1 42.1 %all-to-all-start = ((bf16[256,8,128]{2,1,0:T(8,128)(2,1)}), bf16[256,8,128]{2,1,0:T(8,128)(2,1)S(1)}, u32[]{:S(2)}, u32[]{:S(2)}) async-start(bf16[256,8,128]{2,1,0:T(8,128)(2,1)} %bitcast.11), calls=%async_computation | async-start | bytes 1048576 | tf_op jit(solution)/shard_map/all_to_all | solution.py:208
  26.3 4.9 %copy-start.3 = (s32[1,1024]{1,0:T(1,128)S(1)}, s32[1,1024]{1,0:T(1,128)}, u32[]{:S(2)}) copy-start(s32[1,1024]{1,0:T(1,128)} %refs_0_.3) | copy-start | bytes 12292
  26.3 18.8 %collective-permute-start = (bf16[2048,256]{1,0:T(8,128)(2,1)S(1)}, bf16[2048,256]{1,0:T(8,128)(2,1)}, u32[]{:S(2)}, u32[]{:S(2)}) collective-permute-start(bf16[2048,256]{1,0:T(8,128)(2,1)S(1)} %copy-done), channel_id=1, source_target_pairs={{0,32},{32,0},{1,33},{33,1},{2,34},{34,2},{3,35},{35,3},{4,36},{36... | collective-permute-start | bytes 3145736 | tf_op jit(solution)/shard_map/ppermute | solution.py:207
  30.5 0.7 copy-start.4
  31.2 14.0 %copy-start.1 = (bf16[768,512]{1,0:T(8,128)(2,1)S(1)}, bf16[768,512]{1,0:T(8,128)(2,1)}, u32[]{:S(2)}) copy-start(bf16[768,512]{1,0:T(8,128)(2,1)} %w_first_ref.1) | copy-start | bytes 2359300
  31.2 14.0 %copy-start.2 = (bf16[512,512]{1,0:T(8,128)(2,1)S(1)}, bf16[512,512]{1,0:T(8,128)(2,1)}, u32[]{:S(2)}) copy-start(bf16[512,512]{1,0:T(8,128)(2,1)} %w_second_ref.1) | copy-start | bytes 1572868

commit v5 on v4

v5 whole, which is shorter than its diff:
```python
import math

import jax
import jax.numpy as jnp
from jax import lax
from jax.experimental import pallas as pl
from jax.experimental.pallas import tpu as pltpu
from jax.sharding import Mesh
from jax.sharding import PartitionSpec as P

ALL = ("y", "core", "pair", "side", "z")
GROUPS = ("y", "pair", "z")
FOUR = 4
KEPT = 32
BIG = float(1 << 24)
CAP = 3
ROWS = 8
MIB = 1 << 20
BF = jnp.bfloat16
F32 = jnp.float32


def dot_nt(a, b):
    return lax.dot_general(a, b, (((1,), (1,)), ((), ())), preferred_element_type=F32)


def dot_nn(a, b):
    return lax.dot_general(a, b, (((1,), (0,)), ((), ())), preferred_element_type=F32)


def silu(v):
    half = 0.5 * v
    return half + half * jnp.tanh(half)


def asked_keys(which, shape, groups, item_rows, ids):
    pairs, depth = shape
    holder = lax.shift_right_logical(ids, item_rows.bit_length() - 1)
    slot = lax.broadcasted_iota(jnp.int32, ids.shape, 1)
    key = (slot * item_rows + (ids & (item_rows - 1))).astype(F32)
    core = lax.axis_index("core") ^ (which & 1)
    side = lax.axis_index("side") ^ (which >> 1)
    group = lax.broadcasted_iota(jnp.int32, (groups, 1), 0)
    device = ((group // (pairs * depth)) * 2 + core) * pairs + (group // depth) % pairs
    device = (device * 2 + side) * depth + group % depth
    mine = holder == device
    low = jnp.min(jnp.where(mine, key, BIG), axis=1, keepdims=True)
    high = jnp.max(jnp.where(mine, key, -1.0), axis=1, keepdims=True)
    total = jnp.sum(jnp.where(mine, key, 0.0), axis=1, keepdims=True)
    return key, low, high, total


def ask_kernel(shape, groups, item_rows, query_ref, feature_ref, ids_ref, message_ref, spread_ref):
    ids = ids_ref[...]
    lane = lax.broadcasted_iota(jnp.int32, (groups, 128), 1)
    wanted = jnp.full((groups, 128), -1.0, F32)
    for which in range(FOUR):
        _, low, high, total = asked_keys(which, shape, groups, item_rows, ids)
        middle = total - low - high
        least = jnp.where(high >= 0.0, low, -1.0)
        middle = jnp.where((high > low) & (middle > 0.0), middle, -1.0)
        most = jnp.where(high > low, high, -1.0)
        for j, keys in enumerate((least, middle, most)):
            at = 2 * (which * CAP + j)
            wanted = jnp.where((lane == at) | (lane == at + 1), keys, wanted)
    wanted = wanted.astype(jnp.int32)
    inside = jnp.where(wanted < 0, 2 * item_rows, wanted & (item_rows - 1))
    asked = jnp.where((lane & 1) == 0, lax.shift_right_logical(inside, 8), inside & 255)
    asked = asked.astype(F32)
    spread_ref[pl.ds(ROWS - 2, groups, stride=ROWS), :] = asked
    line = lax.broadcasted_iota(jnp.int32, (ROWS, 128), 0)
    own = jnp.zeros((ROWS, 128), F32)
    at = 0
    for ref in (query_ref, feature_ref):
        for k in range(0, ref.shape[1], 128):
            own = jnp.where(line == at, ref[:, k : k + 128].astype(F32), own)
            at += 1
    spread = spread_ref[...].reshape(groups, ROWS, 128)
    spread = jnp.where((line == ROWS - 2)[None], spread, own[None])
    message_ref[...] = spread.reshape(ROWS * groups, 128).astype(BF)


def place_kernel(
    shape, groups, item_rows, ids_ref, length_ref, logged_ref, prop_ref, facts_ref, chosen_ref
):
    ids = ids_ref[...]
    first = jnp.zeros(ids.shape, F32)
    last = jnp.zeros(ids.shape, F32)
    for which in range(FOUR):
        key, low, high, _ = asked_keys(which, shape, groups, item_rows, ids)
        first = first + jnp.sum(jnp.where(low == key, 1.0, 0.0), axis=0, keepdims=True)
        last = last + jnp.sum(jnp.where(high == key, 1.0, 0.0), axis=0, keepdims=True)
    place = jnp.where(first > 0.0, 0, jnp.where(last > 0.0, 2, 1))
    holder = lax.shift_right_logical(ids, item_rows.bit_length() - 1)
    pairs, depth = shape
    which = ((holder // (2 * depth * pairs)) & 1) ^ lax.axis_index("core")
    which = which + 2 * (((holder // depth) & 1) ^ lax.axis_index("side"))
    place = which * CAP + place
    slot = lax.broadcasted_iota(jnp.int32, ids.shape, 1)
    ones = jnp.ones(ids.shape, F32)
    length = length_ref[0]
    facts_ref[0:1] = place.astype(F32)
    facts_ref[1:2] = jnp.where(slot < length, 1.0, 0.0)
    facts_ref[2:3] = jnp.where(slot == logged_ref[0], 1.0, 0.0)
    facts_ref[3:4] = jnp.log(ones * length.astype(F32)) - jnp.log(
        ones * (prop_ref[0].astype(F32) / 1024.0)
    )
    group_of = (holder // (4 * depth * pairs)) * pairs + (holder // (2 * depth)) % pairs
    group_of = group_of * depth + holder % depth
    group = lax.broadcasted_iota(jnp.int32, chosen_ref.shape, 0)
    chosen_ref[...] = jnp.where(group == group_of, 1.0, 0.0).astype(BF)


def hold_kernel(
    asked_ref, own_ref, second_hbm, third_hbm, fourth_hbm, w_first_ref, w_second_ref, w_score_ref,
    out_ref, lines_ref, second_ref, third_ref, fourth_ref, sems,
):
    copies = (
        None,
        pltpu.make_async_copy(second_hbm, second_ref, sems.at[0]),
        pltpu.make_async_copy(third_hbm, third_ref, sems.at[1]),
        pltpu.make_async_copy(fourth_hbm, fourth_ref, sems.at[2]),
    )
    for copy in copies[1:]:
        copy.start()
    contexts = asked_ref.shape[0] // ROWS
    tables = (own_ref, second_ref, third_ref, fourth_ref)
    item_rows, width = own_ref.shape
    feature_width = w_first_ref.shape[0] - width
    lines_ref[...] = asked_ref[...].astype(F32)
    lines = [lines_ref[pl.ds(k, contexts, stride=ROWS), :] for k in range(ROWS - 1)]
    query_wide = jnp.concatenate(lines[: width // 128], axis=1)
    query = query_wide.astype(BF)
    features = jnp.concatenate(lines[width // 128 : ROWS - 2], axis=1).astype(BF)
    id_parts = lines[ROWS - 2]
    lane = lax.broadcasted_iota(jnp.int32, (contexts, 128), 1)
    chunk = 1024
    peak = jnp.full((contexts, 128), -1e30, F32)
    total = jnp.zeros((contexts, 128), F32)
    out = jnp.zeros((contexts, 128), F32)
    context_part = dot_nn(features, w_first_ref[:feature_width, :])
    context_part = jnp.concatenate([context_part] * CAP, axis=0)
    item = lax.broadcasted_iota(jnp.int32, (CAP * contexts, item_rows), 1)
    w_score = jnp.broadcast_to(w_score_ref[...], (128, w_score_ref.shape[1]))
    for which in range(FOUR):
        if copies[which] is not None:
            copies[which].wait()
        table = tables[which]
        for start in range(0, item_rows, chunk):
            logits = dot_nt(query, table[start : start + chunk, :])
            new = peak
            for k in range(0, chunk, 128):
                new = jnp.maximum(new, logits[:, k : k + 128])
            total = total * jnp.exp(peak - new)
            for k in range(0, chunk, 128):
                total = total + jnp.exp(logits[:, k : k + 128] - new)
            peak = new
        at = 2 * which * CAP
        inside = jnp.concatenate(
            [
                id_parts[:, at + 2 * j : at + 2 * j + 1] * 256.0
                + id_parts[:, at + 2 * j + 1 : at + 2 * j + 2]
                for j in range(CAP)
            ],
            axis=0,
        ).astype(jnp.int32)
        chosen = jnp.where(item == inside, 1.0, 0.0).astype(BF)
        rows = dot_nn(chosen, table[...])
        hidden = silu(dot_nn(rows.astype(BF), w_first_ref[feature_width:, :]) + context_part)
        second = silu(dot_nn(hidden.astype(BF), w_second_ref[...]))
        score = dot_nt(second.astype(BF), w_score)
        for j in range(CAP):
            mine = slice(j * contexts, (j + 1) * contexts)
            gen = jnp.sum(rows[mine] * query_wide, axis=1, keepdims=True)
            place = which * CAP + j
            out = jnp.where(lane == place, score[mine], out)
            out = jnp.where(lane == FOUR * CAP + place, gen, out)
    top = jnp.max(peak, axis=1, keepdims=True)
    total = jnp.sum(total * jnp.exp(peak - top), axis=1, keepdims=True)
    out = jnp.where(lane == 2 * FOUR * CAP, top, jnp.where(lane == 2 * FOUR * CAP + 1, total, out))
    out_ref[...] = out


def own_kernel(total_items, back_ref, chosen_ref, facts_ref, section_ref, weight_ref):
    back = jnp.transpose(back_ref[...])[:KEPT]
    top = back.astype(BF)
    rest = back - top.astype(F32)
    middle = rest.astype(BF)
    low = (rest - middle.astype(F32)).astype(BF)
    found = dot_nn(jnp.concatenate([top, middle, low], axis=0), chosen_ref[...])
    found = found[:KEPT] + found[KEPT : 2 * KEPT] + found[2 * KEPT :]
    at = 2 * FOUR * CAP
    peaks, sums = back[at : at + 1], back[at + 1 : at + 2]
    peak = jnp.max(peaks, axis=1, keepdims=True)
    log_norm = peak + jnp.log(jnp.sum(sums * jnp.exp(peaks - peak), axis=1, keepdims=True))
    place = facts_ref[0:1]
    live = facts_ref[1:2] > 0.0
    score = jnp.zeros(place.shape, F32)
    gen = jnp.zeros(place.shape, F32)
    for k in range(FOUR * CAP):
        score = jnp.where(place == k, found[k : k + 1], score)
        gen = jnp.where(place == k, found[FOUR * CAP + k : FOUR * CAP + k + 1], gen)
    masked = jnp.where(live, score, -1e30)
    rank_peak = jnp.max(masked, axis=1, keepdims=True)
    rank_sum = jnp.sum(jnp.where(live, jnp.exp(masked - rank_peak), 0.0), axis=1, keepdims=True)
    rank_norm = rank_peak + jnp.log(rank_sum)
    section = jnp.where(live, score - rank_norm + gen - log_norm + math.log(total_items), 0.0)
    section_ref[...] = section
    chosen = jnp.sum(jnp.where(facts_ref[2:3] > 0.0, section, 0.0), axis=1, keepdims=True)
    weight_ref[...] = chosen + facts_ref[3:4, :128]


def body(
    query, item_table, context_features, candidates, lengths, logged_slot, logging_prop,
    w_first, w_second, w_score,
):
    item_rows, width = item_table.shape
    slots = candidates.shape[1]
    groups = lax.axis_size(GROUPS)
    shape = (lax.axis_size("pair"), lax.axis_size("z"))
    vmem = pl.BlockSpec(memory_space=pltpu.VMEM)
    smem = pl.BlockSpec(memory_space=pltpu.SMEM)

    third = lax.ppermute(item_table, "side", [(0, 1), (1, 0)])
    message = pl.pallas_call(
        lambda *refs: ask_kernel(shape, groups, item_rows, *refs),
        out_shape=jax.ShapeDtypeStruct((ROWS * groups, 128), BF),
        in_specs=[vmem] * 3,
        out_specs=vmem,
        scratch_shapes=[pltpu.VMEM((ROWS * groups, 128), F32)],
        compiler_params=pltpu.CompilerParams(vmem_limit_bytes=60 * MIB),
        name="ask",
    )(query, context_features, candidates)
    tied_table, message = lax.optimization_barrier((item_table, message))
    second = lax.ppermute(tied_table, "core", [(0, 1), (1, 0)])
    asked = lax.all_to_all(
        message.reshape(groups, ROWS, 128), GROUPS, split_axis=0, concat_axis=0, tiled=True
    ).reshape(ROWS * groups, 128)
    facts, chosen = pl.pallas_call(
        lambda *refs: place_kernel(shape, groups, item_rows, *refs),
        out_shape=(
            jax.ShapeDtypeStruct((8, slots), F32),
            jax.ShapeDtypeStruct((groups, slots), BF),
        ),
        in_specs=[vmem] + [smem] * 3,
        out_specs=(vmem, vmem),
        compiler_params=pltpu.CompilerParams(vmem_limit_bytes=8 * MIB),
        cost_estimate=pl.CostEstimate(flops=20000000000, bytes_accessed=600000, transcendentals=0),
        name="place",
    )(candidates, lengths, logged_slot, logging_prop)
    asked, facts = lax.optimization_barrier((asked, facts))
    fourth = lax.ppermute(third, "core", [(0, 1), (1, 0)])
    answers = pl.pallas_call(
        hold_kernel,
        out_shape=jax.ShapeDtypeStruct((groups, 128), F32),
        in_specs=[vmem] * 2 + [pl.BlockSpec(memory_space=pl.ANY)] * 3 + [vmem] * 3,
        out_specs=vmem,
        scratch_shapes=[
            pltpu.VMEM((ROWS * groups, 128), F32),
            pltpu.VMEM(item_table.shape, BF),
            pltpu.VMEM(item_table.shape, BF),
            pltpu.VMEM(item_table.shape, BF),
            pltpu.SemaphoreType.DMA((3,)),
        ],
        compiler_params=pltpu.CompilerParams(vmem_limit_bytes=51 * MIB),
        name="hold",
    )(asked, item_table, second, third, fourth, w_first, w_second, w_score.reshape(1, -1))
    back = lax.all_to_all(
        answers.reshape(groups, 1, 128), GROUPS, split_axis=0, concat_axis=0, tiled=True
    ).reshape(groups, 128)
    total_items = item_rows * FOUR * groups
    section, weight = pl.pallas_call(
        lambda *refs: own_kernel(total_items, *refs),
        out_shape=(
            jax.ShapeDtypeStruct((1, slots), F32),
            jax.ShapeDtypeStruct((1, 128), F32),
        ),
        in_specs=[vmem] * 3,
        out_specs=(vmem, vmem),
        compiler_params=pltpu.CompilerParams(vmem_limit_bytes=8 * MIB),
        name="own",
    )(back, chosen, facts)
    return section, weight[0, :1]


def solution(mesh):
    split = Mesh(mesh.devices.reshape(8, 2, 2, 2, 8), ALL)
    row, flat = P(ALL, None), P(ALL)
    placed = (row, row, row, row, flat, flat, flat, P(), P(), P())
    return jax.shard_map(
        body, mesh=split, in_specs=placed, out_specs=(row, flat), check_vma=False
    )
```

time: 75.1 us -> 80.4 us (1.071)
  waiting for transfers between devices: 12.9 us -> 6.05 us
  blocking collectives: 21.7 us -> 28.4 us
  Pallas kernels: 10.7 us -> 14 us
  starting transfers between devices: 26.1 us -> 28.8 us
    all_to_all x1, waiting for transfers between devices: 12.9 us -> 6.04 us  [body(): lax.all_to_all(message.reshape(groups, ROWS, 128), GROUPS, split_axis=0,...]
    all_to_all x1, blocking collectives: 21.7 us -> 28.4 us  [body(): lax.all_to_all(answers.reshape(groups, 1, 128), GROUPS, split_axis=0, con...]
    ppermute x1 -> x3, starting transfers between devices: 2.86 us -> 9.15 us  [the longest x1 3.95 us: body(): third = lax.ppermute(item_table, 'side', [(0, 1), (1, 0)])]
    all_to_all x1, starting transfers between devices: 23.2 us -> 19.7 us  [body(): lax.all_to_all(message.reshape(groups, ROWS, 128), GROUPS, split_axis=0,...]
    pallas_call x3, Pallas kernels: 9.62 us -> 12.9 us  [the longest x1 9.62 us: body(): pl.pallas_call(hold_kernel, out_shape=jax.ShapeDtypeStruct((groups, 128),...]
  transfers between devices with their start and end apart: 2 -> 4, of which waited for: 1 -> 1; matrix products, arithmetic and copies ran while one was open for 0% -> 0% of each run, Pallas kernels for 1% -> 4%
where the time goes in v5:
time: 80.4 us; the launch traced here: 80 us
  starting transfers between devices  28.8 us (36%)
  blocking collectives  28.4 us (35%)
  Pallas kernels  14 us (17%)
  waiting for transfers between devices  6.05 us (8%)
  between operations  2.7 us (3%)
    all_to_all x1, blocking collectives, body(): lax.all_to_all(answers.reshape(groups, 1, 128), GROUPS, split_axis=0, con...  28.4 us
    all_to_all x1, starting transfers between devices, body(): lax.all_to_all(message.reshape(groups, ROWS, 128), GROUPS, split_axis=0,...  19.7 us
    pallas_call x1, Pallas kernels, body(): pl.pallas_call(hold_kernel, out_shape=jax.ShapeDtypeStruct((groups, 128),...  9.62 us
    all_to_all x1, waiting for transfers between devices, body(): lax.all_to_all(message.reshape(groups, ROWS, 128), GROUPS, split_axis=0,...  6.04 us
    ppermute x1, starting transfers between devices, body(): third = lax.ppermute(item_table, 'side', [(0, 1), (1, 0)])  3.95 us
    ppermute x1, starting transfers between devices, body(): second = lax.ppermute(tied_table, 'core', [(0, 1), (1, 0)])  3.15 us
    pallas_call x1, Pallas kernels, body(): pl.pallas_call(lambda *refs: ask_kernel(shape, groups, item_rows, *refs),...  2.27 us
    ppermute x1, starting transfers between devices, body(): fourth = lax.ppermute(third, 'core', [(0, 1), (1, 0)])  2.05 us
  transfers between devices with their start and end apart: 4, of which 1 were waited for; matrix products, arithmetic and copies ran while one was open for 0% of the time, Pallas kernels for 4%

profile of v5, /device:TPU:1, one launch (start us, length us, event | category | flops | bytes accessed | tf_op | source)
XLA Modules:
  0.0 80.0 jit_solution(11015403558487116860)
XLA Ops:
  0.6 4.0 %collective-permute-start.1 = (bf16[2048,256]{1,0:T(8,128)(2,1)}, bf16[2048,256]{1,0:T(8,128)(2,1)}, u32[]{:S(2)}, u32[]{:S(2)}) collective-permute-start(bf16[2048,256]{1,0:T(8,128)(2,1)} %own_ref.1), channel_id=1, source_target_pairs={{0,8},{8,0},{1,9},{9,1},{2,10},{10,2},{3,11},{11,3},{4,12},{12,4},... | collective-permute-start | bytes 3145736 | tf_op jit(solution)/shard_map/ppermute | solution.py:224
  4.6 2.3 %ask.1 = bf16[1024,128]{1,0:T(8,128)(2,1)} custom-call(bf16[1,256]{1,0:T(2,128)(2,1)} %refs_0_.2, bf16[1,512]{1,0:T(2,128)(2,1)} %refs_1_.2, s32[1,1024]{1,0:T(1,128)} %refs_0_.3), custom_call_target="tpu_custom_call" | custom-call | tf_op jit(solution)/shard_map/ask/pallas_call | solution.py:225
  6.9 19.7 %all-to-all-start = ((bf16[128,8,128]{2,1,0:T(8,128)(2,1)}), bf16[128,8,128]{2,1,0:T(8,128)(2,1)S(1)}, u32[]{:S(2)}, u32[]{:S(2)}) async-start(bf16[128,8,128]{2,1,0:T(8,128)(2,1)} %bitcast.11), calls=%async_computation | async-start | bytes 524288 | tf_op jit(solution)/shard_map/all_to_all | solution.py:236
  26.6 0.0 copy-start.3
  26.6 3.1 %collective-permute-start = (bf16[2048,256]{1,0:T(8,128)(2,1)}, bf16[2048,256]{1,0:T(8,128)(2,1)}, u32[]{:S(2)}, u32[]{:S(2)}) collective-permute-start(bf16[2048,256]{1,0:T(8,128)(2,1)} %own_ref.1), channel_id=1, source_target_pairs={{0,32},{32,0},{1,33},{33,1},{2,34},{34,2},{3,35},{35,3},{4,36},{36... | collective-permute-start | bytes 3145736 | tf_op jit(solution)/shard_map/ppermute | solution.py:235
  31.7 0.0 copy-start.4
  31.7 0.0 copy-start
  31.7 0.0 copy-start.1
  31.7 0.0 copy-start.2
  31.7 0.0 collective-permute-done.1.third_hbm
  31.7 2.1 %collective-permute-start.2 = (bf16[2048,256]{1,0:T(8,128)(2,1)}, bf16[2048,256]{1,0:T(8,128)(2,1)}, u32[]{:S(2)}, u32[]{:S(2)}) collective-permute-start(bf16[2048,256]{1,0:T(8,128)(2,1)} %collective-permute-done.1.third_hbm), channel_id=1, source_target_pairs={{0,32},{32,0},{1,33},{33,1},{2,34},{34,2},{3,35},{35,3},{4,36},{36... | collective-permute-start | bytes 3145736 | tf_op jit(solution)/shard_map/ppermute | solution.py:252
  33.8 0.0 copy-done.3
  33.8 1.0 %place.1 = (f32[8,1024]{1,0:T(8,128)S(1)}, bf16[128,1024]{1,0:T(8,128)(2,1)S(1)}) custom-call(s32[1,1024]{1,0:T(1,128)S(1)} %copy-done.3, s32[1]{0:T(128)S(6)} %copy.13.refs_1_, s32[1]{0:T(128)S(6)} %copy.14.refs_2_, s32[1]{0:T(128)S(6)} %copy.15.refs_3_), custom_call_target="tpu_custom_call" | custom-call | flops 20000000000 | bytes 600000 | tf_op jit(solution)/shard_map/place/pallas_call | solution.py:239
  34.8 0.0 copy-done.4
  34.9 6.0 %all-to-all-done = bf16[128,8,128]{2,1,0:T(8,128)(2,1)S(1)} async-done(((bf16[128,8,128]{2,1,0:T(8,128)(2,1)}), bf16[128,8,128]{2,1,0:T(8,128)(2,1)S(1)}, u32[]{:S(2)}, u32[]{:S(2)}) %all-to-all-start) | async-done | bytes 262176 | tf_op jit(solution)/shard_map/all_to_all | solution.py:236
  40.9 0.0 collective-permute-done.second_hbm
  40.9 0.0 collective-permute-done.2.fourth_hbm
  40.9 0.0 copy-done
  40.9 0.0 copy-done.1
  40.9 0.0 copy-done.2
  40.9 9.6 %hold.1 = f32[128,128]{1,0:T(8,128)S(1)} custom-call(bf16[1024,128]{1,0:T(8,128)(2,1)S(1)} %bitcast.8, bf16[2048,256]{1,0:T(8,128)(2,1)S(1)} %copy-done, bf16[2048,256]{1,0:T(8,128)(2,1)} %collective-permute-done.second_hbm, bf16[2048,256]{1,0:T(8,128)(2,1)} %collective-permute-done.1.third_hbm, bf16[2048,256]{1,0:T(8,128)(2,1)} %collective-permute-done.2.fourth_hbm, ...), custom_call_target="tpu_custom_call" | custom-call | tf_op jit(solution)/shard_map/hold/pallas_call | solution.py:253
  50.6 28.4 %all_to_all.10 = f32[128,1,128]{2,1,0:T(1,128)S(1)} all-to-all(f32[128,1,128]{2,1,0:T(1,128)S(1)} %bitcast.9), channel_id=1, replica_groups=mesh['y'=8,'core'=2,'pair'=2,'side'=2,'z'=8] {'y','pair','z'}, dimensions={0} | all-to-all | bytes 131072 | tf_op jit(solution)/shard_map/all_to_all | solution.py:268
  79.0 1.0 %own.1 = (f32[1,1024]{1,0:T(1,128)}, f32[1,128]{1,0:T(1,128)}) custom-call(f32[128,128]{1,0:T(8,128)S(1)} %bitcast.10, bf16[128,1024]{1,0:T(8,128)(2,1)S(1)} %get-tuple-element.14.refs_1_, f32[8,1024]{1,0:T(8,128)S(1)} %get-tuple-element.15.refs_2_), custom_call_target="tpu_custom_call" | custom-call | tf_op jit(solution)/shard_map/own/pallas_call | solution.py:272
  (1 shorter events, 0.0 us)
Async XLA Ops:
  0.6 31.1 %collective-permute-start.1 = (bf16[2048,256]{1,0:T(8,128)(2,1)}, bf16[2048,256]{1,0:T(8,128)(2,1)}, u32[]{:S(2)}, u32[]{:S(2)}) collective-permute-start(bf16[2048,256]{1,0:T(8,128)(2,1)} %own_ref.1), channel_id=1, source_target_pairs={{0,8},{8,0},{1,9},{9,1},{2,10},{10,2},{3,11},{11,3},{4,12},{12,4},... | collective-permute-start | bytes 3145736 | tf_op jit(solution)/shard_map/ppermute | solution.py:224
  6.9 34.0 %all-to-all-start = ((bf16[128,8,128]{2,1,0:T(8,128)(2,1)}), bf16[128,8,128]{2,1,0:T(8,128)(2,1)S(1)}, u32[]{:S(2)}, u32[]{:S(2)}) async-start(bf16[128,8,128]{2,1,0:T(8,128)(2,1)} %bitcast.11), calls=%async_computation | async-start | bytes 524288 | tf_op jit(solution)/shard_map/all_to_all | solution.py:236
  26.6 7.2 %copy-start.3 = (s32[1,1024]{1,0:T(1,128)S(1)}, s32[1,1024]{1,0:T(1,128)}, u32[]{:S(2)}) copy-start(s32[1,1024]{1,0:T(1,128)} %refs_0_.3) | copy-start | bytes 12292
  26.6 14.3 %collective-permute-start = (bf16[2048,256]{1,0:T(8,128)(2,1)}, bf16[2048,256]{1,0:T(8,128)(2,1)}, u32[]{:S(2)}, u32[]{:S(2)}) collective-permute-start(bf16[2048,256]{1,0:T(8,128)(2,1)} %own_ref.1), channel_id=1, source_target_pairs={{0,32},{32,0},{1,33},{33,1},{2,34},{34,2},{3,35},{35,3},{4,36},{36... | collective-permute-start | bytes 3145736 | tf_op jit(solution)/shard_map/ppermute | solution.py:235
  31.7 3.2 %copy-start.4 = (bf16[512]{0:T(512)(128)(2,1)S(1)}, bf16[512]{0:T(512)(128)(2,1)}, u32[]{:S(2)}) copy-start(bf16[512]{0:T(512)(128)(2,1)} %param.19) | copy-start | bytes 3076
  31.7 9.2 %copy-start = (bf16[2048,256]{1,0:T(8,128)(2,1)S(1)}, bf16[2048,256]{1,0:T(8,128)(2,1)}, u32[]{:S(2)}) copy-start(bf16[2048,256]{1,0:T(8,128)(2,1)} %own_ref.1) | copy-start | bytes 3145732
  31.7 9.2 %copy-start.1 = (bf16[768,512]{1,0:T(8,128)(2,1)S(1)}, bf16[768,512]{1,0:T(8,128)(2,1)}, u32[]{:S(2)}) copy-start(bf16[768,512]{1,0:T(8,128)(2,1)} %w_first_ref.1) | copy-start | bytes 2359300
  31.7 9.2 %copy-start.2 = (bf16[512,512]{1,0:T(8,128)(2,1)S(1)}, bf16[512,512]{1,0:T(8,128)(2,1)}, u32[]{:S(2)}) copy-start(bf16[512,512]{1,0:T(8,128)(2,1)} %w_second_ref.1) | copy-start | bytes 1572868
  31.7 9.2 %collective-permute-start.2 = (bf16[2048,256]{1,0:T(8,128)(2,1)}, bf16[2048,256]{1,0:T(8,128)(2,1)}, u32[]{:S(2)}, u32[]{:S(2)}) collective-permute-start(bf16[2048,256]{1,0:T(8,128)(2,1)} %collective-permute-done.1.third_hbm), channel_id=1, source_target_pairs={{0,32},{32,0},{1,33},{33,1},{2,34},{34,2},{3,35},{35,3},{4,36},{36... | collective-permute-start | bytes 3145736 | tf_op jit(solution)/shard_map/ppermute | solution.py:252

commit v6 on v4

--- a/solution.py
+++ b/solution.py
@@ -9,7 +9,7 @@
 from jax.sharding import PartitionSpec as P
 
 ALL = ("y", "core", "x", "z")
-CHIPS = ("y", "x", "z")
+CHIPS = ("z", "y", "x")
 BIG = float(1 << 24)
 CAP = 3
 ROWS = 8
@@ -37,7 +37,9 @@
     key = (slot * item_rows + (ids & (item_rows - 1))).astype(F32)
     core = lax.axis_index("core") ^ which
     chip = lax.broadcasted_iota(jnp.int32, (chips, 1), 0)
-    device = (chip // plane) * (2 * plane) + core * plane + chip % plane
+    rows, columns, depth = plane
+    x, y, z = chip % columns, (chip // columns) % rows, chip // (columns * rows)
+    device = ((y * 2 + core) * columns + x) * depth + z
     mine = holder == device
     low = jnp.min(jnp.where(mine, key, BIG), axis=1, keepdims=True)
     high = jnp.max(jnp.where(mine, key, -1.0), axis=1, keepdims=True)
@@ -87,7 +89,8 @@
         last = last + jnp.sum(jnp.where(high == key, 1.0, 0.0), axis=0, keepdims=True)
     place = jnp.where(first > 0.0, 0, jnp.where(last > 0.0, 2, 1))
     holder = lax.shift_right_logical(ids, item_rows.bit_length() - 1)
-    place = (((holder // plane) & 1) ^ lax.axis_index("core")) * CAP + place
+    rows, columns, depth = plane
+    place = (((holder // (columns * depth)) & 1) ^ lax.axis_index("core")) * CAP + place
     slot = lax.broadcasted_iota(jnp.int32, ids.shape, 1)
     ones = jnp.ones(ids.shape, F32)
     length = length_ref[0]
@@ -97,7 +100,8 @@
     facts_ref[3:4] = jnp.log(ones * length.astype(F32)) - jnp.log(
         ones * (prop_ref[0].astype(F32) / 1024.0)
     )
-    chip_of = (holder // (2 * plane)) * plane + holder % plane
+    chip_of = (holder % depth) * rows + holder // (2 * columns * depth)
+    chip_of = chip_of * columns + (holder // depth) % columns
     chip = lax.broadcasted_iota(jnp.int32, chosen_ref.shape, 0)
     chosen_ref[...] = jnp.where(chip == chip_of, 1.0, 0.0).astype(BF)
 
@@ -191,7 +195,7 @@
     item_rows, width = item_table.shape
     slots = candidates.shape[1]
     chips = lax.axis_size(CHIPS)
-    plane = lax.axis_size(("x", "z"))
+    plane = (lax.axis_size("y"), lax.axis_size("x"), lax.axis_size("z"))
     vmem = pl.BlockSpec(memory_space=pltpu.VMEM)
     smem = pl.BlockSpec(memory_space=pltpu.SMEM)
 

time: 75.1 us -> 75 us (level)
  blocking collectives: 21.7 us -> 22.9 us
  waiting for transfers between devices: 12.9 us -> 11.8 us
    all_to_all x1, blocking collectives: 21.7 us -> 22.9 us  [body(): lax.all_to_all(answers.reshape(chips, 1, 128), CHIPS, split_axis=0, conca...]
    all_to_all x1, waiting for transfers between devices: 12.9 us -> 11.8 us  [body(): lax.all_to_all(message.reshape(chips, ROWS, 128), CHIPS, split_axis=0, co...]
  transfers between devices with their start and end apart: 2 -> 2, of which waited for: 1 -> 1; matrix products, arithmetic and copies ran while one was open for 0% -> 0% of each run, Pallas kernels for 1% -> 2%
where the time goes in v6:
time: 75 us; the launch traced here: 74.3 us
  starting transfers between devices  26.1 us (35%)
  blocking collectives  22.9 us (31%)
  waiting for transfers between devices  11.8 us (16%)
  Pallas kernels  10.7 us (14%)
  between operations  2.68 us (4%)
    all_to_all x1, starting transfers between devices, body(): lax.all_to_all(message.reshape(chips, ROWS, 128), CHIPS, split_axis=0, co...  23.2 us
    all_to_all x1, blocking collectives, body(): lax.all_to_all(answers.reshape(chips, 1, 128), CHIPS, split_axis=0, conca...  22.9 us
    all_to_all x1, waiting for transfers between devices, body(): lax.all_to_all(message.reshape(chips, ROWS, 128), CHIPS, split_axis=0, co...  11.8 us
    pallas_call x1, Pallas kernels, body(): pl.pallas_call(hold_kernel, out_shape=jax.ShapeDtypeStruct((chips, 128),...  6.06 us
    ppermute x1, starting transfers between devices, body(): other_table = lax.ppermute(item_table, 'core', [(0, 1), (1, 0)])  2.86 us
    pallas_call x1, Pallas kernels, body(): pl.pallas_call(lambda *refs: ask_kernel(plane, chips, item_rows, *refs),...  2.52 us
  transfers between devices with their start and end apart: 2, of which 1 were waited for; matrix products, arithmetic and copies ran while one was open for 0% of the time, Pallas kernels for 2%

profile of v6, /device:TPU:1, one launch (start us, length us, event | category | flops | bytes accessed | tf_op | source)
XLA Modules:
  0.0 74.3 jit_solution(14860053691060919906)
XLA Ops:
  0.6 0.0 copy-start
  0.6 2.5 %ask.1 = bf16[2048,128]{1,0:T(8,128)(2,1)} custom-call(bf16[1,256]{1,0:T(2,128)(2,1)} %refs_0_.2, bf16[1,512]{1,0:T(2,128)(2,1)} %refs_1_.2, s32[1,1024]{1,0:T(1,128)} %refs_0_.3), custom_call_target="tpu_custom_call" | custom-call | tf_op jit(solution)/shard_map/ask/pallas_call | solution.py:202
  3.2 23.2 %all-to-all-start = ((bf16[256,8,128]{2,1,0:T(8,128)(2,1)}), bf16[256,8,128]{2,1,0:T(8,128)(2,1)S(1)}, u32[]{:S(2)}, u32[]{:S(2)}) async-start(bf16[256,8,128]{2,1,0:T(8,128)(2,1)} %bitcast.11), calls=%async_computation | async-start | bytes 1048576 | tf_op jit(solution)/shard_map/all_to_all | solution.py:212
  26.4 0.0 copy-done
  26.4 0.0 copy-start.3
  26.4 2.9 %collective-permute-start = (bf16[2048,256]{1,0:T(8,128)(2,1)S(1)}, bf16[2048,256]{1,0:T(8,128)(2,1)}, u32[]{:S(2)}, u32[]{:S(2)}) collective-permute-start(bf16[2048,256]{1,0:T(8,128)(2,1)S(1)} %copy-done), channel_id=1, source_target_pairs={{0,32},{32,0},{1,33},{33,1},{2,34},{34,2},{3,35},{35,3},{4,36},{36... | collective-permute-start | bytes 3145736 | tf_op jit(solution)/shard_map/ppermute | solution.py:211
  30.6 0.0 copy-start.4
  31.2 0.0 copy-done.4
  31.2 0.0 copy-done.3
  31.3 0.0 copy-start.1
  31.3 0.0 copy-start.2
  31.3 1.1 %place.1 = (f32[8,1024]{1,0:T(8,128)S(1)}, bf16[256,1024]{1,0:T(8,128)(2,1)S(1)}) custom-call(s32[1,1024]{1,0:T(1,128)S(1)} %copy-done.3, s32[1]{0:T(128)S(6)} %copy.13.refs_1_, s32[1]{0:T(128)S(6)} %copy.14.refs_2_, s32[1]{0:T(128)S(6)} %copy.15.refs_3_), custom_call_target="tpu_custom_call" | custom-call | flops 20000000000 | bytes 600000 | tf_op jit(solution)/shard_map/place/pallas_call | solution.py:215
  32.4 11.8 %all-to-all-done = bf16[256,8,128]{2,1,0:T(8,128)(2,1)S(1)} async-done(((bf16[256,8,128]{2,1,0:T(8,128)(2,1)}), bf16[256,8,128]{2,1,0:T(8,128)(2,1)S(1)}, u32[]{:S(2)}, u32[]{:S(2)}) %all-to-all-start) | async-done | bytes 524320 | tf_op jit(solution)/shard_map/all_to_all | solution.py:212
  44.2 0.0 collective-permute-done.other_hbm
  44.2 0.0 copy-done.1
  44.2 0.0 copy-done.2
  44.2 6.1 %hold.1 = f32[256,128]{1,0:T(8,128)S(1)} custom-call(bf16[2048,128]{1,0:T(8,128)(2,1)S(1)} %bitcast.8, bf16[2048,256]{1,0:T(8,128)(2,1)S(1)} %copy-done, bf16[2048,256]{1,0:T(8,128)(2,1)} %collective-permute-done.other_hbm, bf16[768,512]{1,0:T(8,128)(2,1)S(1)} %copy-done.1, bf16[512,512]{1,0:T(8,128)(2,1)S(1)} %copy-done.2, ...), custom_call_target="tpu_custom_call" | custom-call | tf_op jit(solution)/shard_map/hold/pallas_call | solution.py:228
  50.3 22.9 %all_to_all.10 = f32[256,1,128]{2,1,0:T(1,128)S(1)} all-to-all(f32[256,1,128]{2,1,0:T(1,128)S(1)} %bitcast.9), channel_id=1, replica_groups=mesh['y'=8,'core'=2,'x'=4,'z'=8] {'z','y','x'}, dimensions={0} | all-to-all | bytes 262144 | tf_op jit(solution)/shard_map/all_to_all | solution.py:241
  73.2 1.0 %own.1 = (f32[1,1024]{1,0:T(1,128)}, f32[1,128]{1,0:T(1,128)}) custom-call(f32[256,128]{1,0:T(8,128)S(1)} %bitcast.10, bf16[256,1024]{1,0:T(8,128)(2,1)S(1)} %get-tuple-element.10.refs_1_, f32[8,1024]{1,0:T(8,128)S(1)} %get-tuple-element.11.refs_2_), custom_call_target="tpu_custom_call" | custom-call | tf_op jit(solution)/shard_map/own/pallas_call | solution.py:245
  (1 shorter events, 0.0 us)
Async XLA Ops:
  0.6 25.7 %copy-start = (bf16[2048,256]{1,0:T(8,128)(2,1)S(1)}, bf16[2048,256]{1,0:T(8,128)(2,1)}, u32[]{:S(2)}) copy-start(bf16[2048,256]{1,0:T(8,128)(2,1)} %own_ref.1) | copy-start | bytes 3145732
  3.2 41.1 %all-to-all-start = ((bf16[256,8,128]{2,1,0:T(8,128)(2,1)}), bf16[256,8,128]{2,1,0:T(8,128)(2,1)S(1)}, u32[]{:S(2)}, u32[]{:S(2)}) async-start(bf16[256,8,128]{2,1,0:T(8,128)(2,1)} %bitcast.11), calls=%async_computation | async-start | bytes 1048576 | tf_op jit(solution)/shard_map/all_to_all | solution.py:212
  26.4 4.9 %copy-start.3 = (s32[1,1024]{1,0:T(1,128)S(1)}, s32[1,1024]{1,0:T(1,128)}, u32[]{:S(2)}) copy-start(s32[1,1024]{1,0:T(1,128)} %refs_0_.3) | copy-start | bytes 12292
  26.4 17.8 %collective-permute-start = (bf16[2048,256]{1,0:T(8,128)(2,1)S(1)}, bf16[2048,256]{1,0:T(8,128)(2,1)}, u32[]{:S(2)}, u32[]{:S(2)}) collective-permute-start(bf16[2048,256]{1,0:T(8,128)(2,1)S(1)} %copy-done), channel_id=1, source_target_pairs={{0,32},{32,0},{1,33},{33,1},{2,34},{34,2},{3,35},{35,3},{4,36},{36... | collective-permute-start | bytes 3145736 | tf_op jit(solution)/shard_map/ppermute | solution.py:211
  30.6 0.7 copy-start.4
  31.3 13.0 %copy-start.1 = (bf16[768,512]{1,0:T(8,128)(2,1)S(1)}, bf16[768,512]{1,0:T(8,128)(2,1)}, u32[]{:S(2)}) copy-start(bf16[768,512]{1,0:T(8,128)(2,1)} %w_first_ref.1) | copy-start | bytes 2359300
  31.3 13.0 %copy-start.2 = (bf16[512,512]{1,0:T(8,128)(2,1)S(1)}, bf16[512,512]{1,0:T(8,128)(2,1)}, u32[]{:S(2)}) copy-start(bf16[512,512]{1,0:T(8,128)(2,1)} %w_second_ref.1) | copy-start | bytes 1572868

commit v7 on v6

--- a/solution.py
+++ b/solution.py
@@ -110,8 +110,15 @@
     asked_ref, own_ref, other_hbm, w_first_ref, w_second_ref, w_score_ref,
     out_ref, lines_ref, other_ref, other_sem,
 ):
-    other_copy = pltpu.make_async_copy(other_hbm, other_ref, other_sem)
-    other_copy.start()
+    half = other_ref.shape[0] // 2
+    other_copies = [
+        pltpu.make_async_copy(
+            other_hbm.at[pl.ds(k * half, half)], other_ref.at[pl.ds(k * half, half)], other_sem.at[k]
+        )
+        for k in range(2)
+    ]
+    for copy in other_copies:
+        copy.start()
     contexts = asked_ref.shape[0] // ROWS
     tables = (own_ref, other_ref)
     item_rows, width = own_ref.shape
@@ -132,7 +139,8 @@
     w_score = jnp.broadcast_to(w_score_ref[...], (128, w_score_ref.shape[1]))
     for core in range(2):
         if core == 1:
-            other_copy.wait()
+            for copy in other_copies:
+                copy.wait()
         for start in range(0, item_rows, chunk):
             logits = dot_nt(query, tables[core][start : start + chunk, :])
             new = peak
@@ -233,7 +241,7 @@
         scratch_shapes=[
             pltpu.VMEM((ROWS * chips, 128), F32),
             pltpu.VMEM(item_table.shape, BF),
-            pltpu.SemaphoreType.DMA,
+            pltpu.SemaphoreType.DMA((2,)),
         ],
         compiler_params=pltpu.CompilerParams(vmem_limit_bytes=51 * MIB),
         name="hold",

time: 75 us -> 75 us (level)
  no operation moved by 1% of the time
where the time goes in v7:
time: 75 us; the launch traced here: 74.3 us
  starting transfers between devices  26.1 us (35%)
  blocking collectives  22.9 us (31%)
  waiting for transfers between devices  11.8 us (16%)
  Pallas kernels  10.7 us (14%)
  between operations  2.68 us (4%)
    all_to_all x1, starting transfers between devices, body(): lax.all_to_all(message.reshape(chips, ROWS, 128), CHIPS, split_axis=0, co...  23.2 us
    all_to_all x1, blocking collectives, body(): lax.all_to_all(answers.reshape(chips, 1, 128), CHIPS, split_axis=0, conca...  22.9 us
    all_to_all x1, waiting for transfers between devices, body(): lax.all_to_all(message.reshape(chips, ROWS, 128), CHIPS, split_axis=0, co...  11.8 us
    pallas_call x1, Pallas kernels, body(): pl.pallas_call(hold_kernel, out_shape=jax.ShapeDtypeStruct((chips, 128),...  6.07 us
    ppermute x1, starting transfers between devices, body(): other_table = lax.ppermute(item_table, 'core', [(0, 1), (1, 0)])  2.86 us
    pallas_call x1, Pallas kernels, body(): pl.pallas_call(lambda *refs: ask_kernel(plane, chips, item_rows, *refs),...  2.52 us
  transfers between devices with their start and end apart: 2, of which 1 were waited for; matrix products, arithmetic and copies ran while one was open for 0% of the time, Pallas kernels for 2%

profile of v7, /device:TPU:1, one launch (start us, length us, event | category | flops | bytes accessed | tf_op | source)
XLA Modules:
  0.0 74.3 jit_solution(12810172794979868455)
XLA Ops:
  0.6 0.0 copy-start
  0.6 2.5 %ask.1 = bf16[2048,128]{1,0:T(8,128)(2,1)} custom-call(bf16[1,256]{1,0:T(2,128)(2,1)} %refs_0_.2, bf16[1,512]{1,0:T(2,128)(2,1)} %refs_1_.2, s32[1,1024]{1,0:T(1,128)} %refs_0_.3), custom_call_target="tpu_custom_call" | custom-call | tf_op jit(solution)/shard_map/ask/pallas_call | solution.py:210
  3.2 23.2 %all-to-all-start = ((bf16[256,8,128]{2,1,0:T(8,128)(2,1)}), bf16[256,8,128]{2,1,0:T(8,128)(2,1)S(1)}, u32[]{:S(2)}, u32[]{:S(2)}) async-start(bf16[256,8,128]{2,1,0:T(8,128)(2,1)} %bitcast.11), calls=%async_computation | async-start | bytes 1048576 | tf_op jit(solution)/shard_map/all_to_all | solution.py:220
  26.4 0.0 copy-done
  26.4 0.0 copy-start.3
  26.4 2.9 %collective-permute-start = (bf16[2048,256]{1,0:T(8,128)(2,1)S(1)}, bf16[2048,256]{1,0:T(8,128)(2,1)}, u32[]{:S(2)}, u32[]{:S(2)}) collective-permute-start(bf16[2048,256]{1,0:T(8,128)(2,1)S(1)} %copy-done), channel_id=1, source_target_pairs={{0,32},{32,0},{1,33},{33,1},{2,34},{34,2},{3,35},{35,3},{4,36},{36... | collective-permute-start | bytes 3145736 | tf_op jit(solution)/shard_map/ppermute | solution.py:219
  30.6 0.0 copy-start.4
  31.2 0.0 copy-done.4
  31.2 0.0 copy-done.3
  31.3 0.0 copy-start.1
  31.3 0.0 copy-start.2
  31.3 1.1 %place.1 = (f32[8,1024]{1,0:T(8,128)S(1)}, bf16[256,1024]{1,0:T(8,128)(2,1)S(1)}) custom-call(s32[1,1024]{1,0:T(1,128)S(1)} %copy-done.3, s32[1]{0:T(128)S(6)} %copy.13.refs_1_, s32[1]{0:T(128)S(6)} %copy.14.refs_2_, s32[1]{0:T(128)S(6)} %copy.15.refs_3_), custom_call_target="tpu_custom_call" | custom-call | flops 20000000000 | bytes 600000 | tf_op jit(solution)/shard_map/place/pallas_call | solution.py:223
  32.4 11.8 %all-to-all-done = bf16[256,8,128]{2,1,0:T(8,128)(2,1)S(1)} async-done(((bf16[256,8,128]{2,1,0:T(8,128)(2,1)}), bf16[256,8,128]{2,1,0:T(8,128)(2,1)S(1)}, u32[]{:S(2)}, u32[]{:S(2)}) %all-to-all-start) | async-done | bytes 524320 | tf_op jit(solution)/shard_map/all_to_all | solution.py:220
  44.2 0.0 collective-permute-done.other_hbm
  44.2 0.0 copy-done.1
  44.2 0.0 copy-done.2
  44.2 6.1 %hold.1 = f32[256,128]{1,0:T(8,128)S(1)} custom-call(bf16[2048,128]{1,0:T(8,128)(2,1)S(1)} %bitcast.8, bf16[2048,256]{1,0:T(8,128)(2,1)S(1)} %copy-done, bf16[2048,256]{1,0:T(8,128)(2,1)} %collective-permute-done.other_hbm, bf16[768,512]{1,0:T(8,128)(2,1)S(1)} %copy-done.1, bf16[512,512]{1,0:T(8,128)(2,1)S(1)} %copy-done.2, ...), custom_call_target="tpu_custom_call" | custom-call | tf_op jit(solution)/shard_map/hold/pallas_call | solution.py:236
  50.3 22.9 %all_to_all.10 = f32[256,1,128]{2,1,0:T(1,128)S(1)} all-to-all(f32[256,1,128]{2,1,0:T(1,128)S(1)} %bitcast.9), channel_id=1, replica_groups=mesh['y'=8,'core'=2,'x'=4,'z'=8] {'z','y','x'}, dimensions={0} | all-to-all | bytes 262144 | tf_op jit(solution)/shard_map/all_to_all | solution.py:249
  73.3 1.0 %own.1 = (f32[1,1024]{1,0:T(1,128)}, f32[1,128]{1,0:T(1,128)}) custom-call(f32[256,128]{1,0:T(8,128)S(1)} %bitcast.10, bf16[256,1024]{1,0:T(8,128)(2,1)S(1)} %get-tuple-element.10.refs_1_, f32[8,1024]{1,0:T(8,128)S(1)} %get-tuple-element.11.refs_2_), custom_call_target="tpu_custom_call" | custom-call | tf_op jit(solution)/shard_map/own/pallas_call | solution.py:253
  (1 shorter events, 0.0 us)
Async XLA Ops:
  0.6 25.7 %copy-start = (bf16[2048,256]{1,0:T(8,128)(2,1)S(1)}, bf16[2048,256]{1,0:T(8,128)(2,1)}, u32[]{:S(2)}) copy-start(bf16[2048,256]{1,0:T(8,128)(2,1)} %own_ref.1) | copy-start | bytes 3145732
  3.2 41.1 %all-to-all-start = ((bf16[256,8,128]{2,1,0:T(8,128)(2,1)}), bf16[256,8,128]{2,1,0:T(8,128)(2,1)S(1)}, u32[]{:S(2)}, u32[]{:S(2)}) async-start(bf16[256,8,128]{2,1,0:T(8,128)(2,1)} %bitcast.11), calls=%async_computation | async-start | bytes 1048576 | tf_op jit(solution)/shard_map/all_to_all | solution.py:220
  26.4 4.9 %copy-start.3 = (s32[1,1024]{1,0:T(1,128)S(1)}, s32[1,1024]{1,0:T(1,128)}, u32[]{:S(2)}) copy-start(s32[1,1024]{1,0:T(1,128)} %refs_0_.3) | copy-start | bytes 12292
  26.4 17.8 %collective-permute-start = (bf16[2048,256]{1,0:T(8,128)(2,1)S(1)}, bf16[2048,256]{1,0:T(8,128)(2,1)}, u32[]{:S(2)}, u32[]{:S(2)}) collective-permute-start(bf16[2048,256]{1,0:T(8,128)(2,1)S(1)} %copy-done), channel_id=1, source_target_pairs={{0,32},{32,0},{1,33},{33,1},{2,34},{34,2},{3,35},{35,3},{4,36},{36... | collective-permute-start | bytes 3145736 | tf_op jit(solution)/shard_map/ppermute | solution.py:219
  30.6 0.7 copy-start.4
  31.3 13.0 %copy-start.1 = (bf16[768,512]{1,0:T(8,128)(2,1)S(1)}, bf16[768,512]{1,0:T(8,128)(2,1)}, u32[]{:S(2)}) copy-start(bf16[768,512]{1,0:T(8,128)(2,1)} %w_first_ref.1) | copy-start | bytes 2359300
  31.3 13.0 %copy-start.2 = (bf16[512,512]{1,0:T(8,128)(2,1)S(1)}, bf16[512,512]{1,0:T(8,128)(2,1)}, u32[]{:S(2)}) copy-start(bf16[512,512]{1,0:T(8,128)(2,1)} %w_second_ref.1) | copy-start | bytes 1572868

commit v8 on v6

--- a/solution.py
+++ b/solution.py
@@ -142,6 +142,7 @@
             for k in range(0, chunk, 128):
                 total = total + jnp.exp(logits[:, k : k + 128] - new)
             peak = new
+        found = []
         for j in range(CAP):
             place = core * CAP + j
             inside = id_parts[:, 2 * place : 2 * place + 1] * 256.0
@@ -149,11 +150,13 @@
             chosen = jnp.where(item == inside, 1.0, 0.0).astype(BF)
             rows = dot_nn(chosen, tables[core][...])
             gen = jnp.sum(rows * query_wide, axis=1, keepdims=True)
-            hidden = silu(dot_nn(rows.astype(BF), w_first_ref[feature_width:, :]) + context_part)
+            out = jnp.where(lane == 2 * CAP + place, gen, out)
+            found.append(rows.astype(BF))
+        for j in range(CAP):
+            hidden = silu(dot_nn(found[j], w_first_ref[feature_width:, :]) + context_part)
             second = silu(dot_nn(hidden.astype(BF), w_second_ref[...]))
             score = dot_nt(second.astype(BF), w_score)
-            out = jnp.where(lane == place, score, out)
-            out = jnp.where(lane == 2 * CAP + place, gen, out)
+            out = jnp.where(lane == core * CAP + j, score, out)
     top = jnp.max(peak, axis=1, keepdims=True)
     total = jnp.sum(total * jnp.exp(peak - top), axis=1, keepdims=True)
     out = jnp.where(lane == 4 * CAP, top, jnp.where(lane == 4 * CAP + 1, total, out))

time: 75 us -> 74.6 us (level)
  no operation moved by 1% of the time
where the time goes in v8:
time: 74.6 us; the launch traced here: 73.9 us
  starting transfers between devices  26.1 us (35%)
  blocking collectives  22.9 us (31%)
  waiting for transfers between devices  11.8 us (16%)
  Pallas kernels  10.3 us (14%)
  between operations  2.68 us (4%)
    all_to_all x1, starting transfers between devices, body(): lax.all_to_all(message.reshape(chips, ROWS, 128), CHIPS, split_axis=0, co...  23.2 us
    all_to_all x1, blocking collectives, body(): lax.all_to_all(answers.reshape(chips, 1, 128), CHIPS, split_axis=0, conca...  22.9 us
    all_to_all x1, waiting for transfers between devices, body(): lax.all_to_all(message.reshape(chips, ROWS, 128), CHIPS, split_axis=0, co...  11.8 us
    pallas_call x1, Pallas kernels, body(): pl.pallas_call(hold_kernel, out_shape=jax.ShapeDtypeStruct((chips, 128),...  5.65 us
    ppermute x1, starting transfers between devices, body(): other_table = lax.ppermute(item_table, 'core', [(0, 1), (1, 0)])  2.86 us
    pallas_call x1, Pallas kernels, body(): pl.pallas_call(lambda *refs: ask_kernel(plane, chips, item_rows, *refs),...  2.52 us
  transfers between devices with their start and end apart: 2, of which 1 were waited for; matrix products, arithmetic and copies ran while one was open for 0% of the time, Pallas kernels for 2%

profile of v8, /device:TPU:1, one launch (start us, length us, event | category | flops | bytes accessed | tf_op | source)
XLA Modules:
  0.0 73.9 jit_solution(17380068568801366595)
XLA Ops:
  0.6 0.0 copy-start
  0.6 2.5 %ask.1 = bf16[2048,128]{1,0:T(8,128)(2,1)} custom-call(bf16[1,256]{1,0:T(2,128)(2,1)} %refs_0_.2, bf16[1,512]{1,0:T(2,128)(2,1)} %refs_1_.2, s32[1,1024]{1,0:T(1,128)} %refs_0_.3), custom_call_target="tpu_custom_call" | custom-call | tf_op jit(solution)/shard_map/ask/pallas_call | solution.py:205
  3.2 23.2 %all-to-all-start = ((bf16[256,8,128]{2,1,0:T(8,128)(2,1)}), bf16[256,8,128]{2,1,0:T(8,128)(2,1)S(1)}, u32[]{:S(2)}, u32[]{:S(2)}) async-start(bf16[256,8,128]{2,1,0:T(8,128)(2,1)} %bitcast.11), calls=%async_computation | async-start | bytes 1048576 | tf_op jit(solution)/shard_map/all_to_all | solution.py:215
  26.4 0.0 copy-done
  26.4 0.0 copy-start.3
  26.4 2.9 %collective-permute-start = (bf16[2048,256]{1,0:T(8,128)(2,1)S(1)}, bf16[2048,256]{1,0:T(8,128)(2,1)}, u32[]{:S(2)}, u32[]{:S(2)}) collective-permute-start(bf16[2048,256]{1,0:T(8,128)(2,1)S(1)} %copy-done), channel_id=1, source_target_pairs={{0,32},{32,0},{1,33},{33,1},{2,34},{34,2},{3,35},{35,3},{4,36},{36... | collective-permute-start | bytes 3145736 | tf_op jit(solution)/shard_map/ppermute | solution.py:214
  30.6 0.0 copy-start.4
  31.2 0.0 copy-done.4
  31.2 0.0 copy-done.3
  31.3 0.0 copy-start.1
  31.3 0.0 copy-start.2
  31.3 1.1 %place.1 = (f32[8,1024]{1,0:T(8,128)S(1)}, bf16[256,1024]{1,0:T(8,128)(2,1)S(1)}) custom-call(s32[1,1024]{1,0:T(1,128)S(1)} %copy-done.3, s32[1]{0:T(128)S(6)} %copy.13.refs_1_, s32[1]{0:T(128)S(6)} %copy.14.refs_2_, s32[1]{0:T(128)S(6)} %copy.15.refs_3_), custom_call_target="tpu_custom_call" | custom-call | flops 20000000000 | bytes 600000 | tf_op jit(solution)/shard_map/place/pallas_call | solution.py:218
  32.4 11.8 %all-to-all-done = bf16[256,8,128]{2,1,0:T(8,128)(2,1)S(1)} async-done(((bf16[256,8,128]{2,1,0:T(8,128)(2,1)}), bf16[256,8,128]{2,1,0:T(8,128)(2,1)S(1)}, u32[]{:S(2)}, u32[]{:S(2)}) %all-to-all-start) | async-done | bytes 524320 | tf_op jit(solution)/shard_map/all_to_all | solution.py:215
  44.2 0.0 collective-permute-done.other_hbm
  44.2 0.0 copy-done.1
  44.2 0.0 copy-done.2
  44.2 5.7 %hold.1 = f32[256,128]{1,0:T(8,128)S(1)} custom-call(bf16[2048,128]{1,0:T(8,128)(2,1)S(1)} %bitcast.8, bf16[2048,256]{1,0:T(8,128)(2,1)S(1)} %copy-done, bf16[2048,256]{1,0:T(8,128)(2,1)} %collective-permute-done.other_hbm, bf16[768,512]{1,0:T(8,128)(2,1)S(1)} %copy-done.1, bf16[512,512]{1,0:T(8,128)(2,1)S(1)} %copy-done.2, ...), custom_call_target="tpu_custom_call" | custom-call | tf_op jit(solution)/shard_map/hold/pallas_call | solution.py:231
  49.9 22.9 %all_to_all.10 = f32[256,1,128]{2,1,0:T(1,128)S(1)} all-to-all(f32[256,1,128]{2,1,0:T(1,128)S(1)} %bitcast.9), channel_id=1, replica_groups=mesh['y'=8,'core'=2,'x'=4,'z'=8] {'z','y','x'}, dimensions={0} | all-to-all | bytes 262144 | tf_op jit(solution)/shard_map/all_to_all | solution.py:244
  72.8 1.0 %own.1 = (f32[1,1024]{1,0:T(1,128)}, f32[1,128]{1,0:T(1,128)}) custom-call(f32[256,128]{1,0:T(8,128)S(1)} %bitcast.10, bf16[256,1024]{1,0:T(8,128)(2,1)S(1)} %get-tuple-element.10.refs_1_, f32[8,1024]{1,0:T(8,128)S(1)} %get-tuple-element.11.refs_2_), custom_call_target="tpu_custom_call" | custom-call | tf_op jit(solution)/shard_map/own/pallas_call | solution.py:248
  (1 shorter events, 0.0 us)
Async XLA Ops:
  0.6 25.7 %copy-start = (bf16[2048,256]{1,0:T(8,128)(2,1)S(1)}, bf16[2048,256]{1,0:T(8,128)(2,1)}, u32[]{:S(2)}) copy-start(bf16[2048,256]{1,0:T(8,128)(2,1)} %own_ref.1) | copy-start | bytes 3145732
  3.2 41.1 %all-to-all-start = ((bf16[256,8,128]{2,1,0:T(8,128)(2,1)}), bf16[256,8,128]{2,1,0:T(8,128)(2,1)S(1)}, u32[]{:S(2)}, u32[]{:S(2)}) async-start(bf16[256,8,128]{2,1,0:T(8,128)(2,1)} %bitcast.11), calls=%async_computation | async-start | bytes 1048576 | tf_op jit(solution)/shard_map/all_to_all | solution.py:215
  26.4 4.9 %copy-start.3 = (s32[1,1024]{1,0:T(1,128)S(1)}, s32[1,1024]{1,0:T(1,128)}, u32[]{:S(2)}) copy-start(s32[1,1024]{1,0:T(1,128)} %refs_0_.3) | copy-start | bytes 12292
  26.4 17.8 %collective-permute-start = (bf16[2048,256]{1,0:T(8,128)(2,1)S(1)}, bf16[2048,256]{1,0:T(8,128)(2,1)}, u32[]{:S(2)}, u32[]{:S(2)}) collective-permute-start(bf16[2048,256]{1,0:T(8,128)(2,1)S(1)} %copy-done), channel_id=1, source_target_pairs={{0,32},{32,0},{1,33},{33,1},{2,34},{34,2},{3,35},{35,3},{4,36},{36... | collective-permute-start | bytes 3145736 | tf_op jit(solution)/shard_map/ppermute | solution.py:214
  30.6 0.7 copy-start.4
  31.3 13.0 %copy-start.1 = (bf16[768,512]{1,0:T(8,128)(2,1)S(1)}, bf16[768,512]{1,0:T(8,128)(2,1)}, u32[]{:S(2)}) copy-start(bf16[768,512]{1,0:T(8,128)(2,1)} %w_first_ref.1) | copy-start | bytes 2359300
  31.3 13.0 %copy-start.2 = (bf16[512,512]{1,0:T(8,128)(2,1)S(1)}, bf16[512,512]{1,0:T(8,128)(2,1)}, u32[]{:S(2)}) copy-start(bf16[512,512]{1,0:T(8,128)(2,1)} %w_second_ref.1) | copy-start | bytes 1572868

commit v9 on v8

--- a/solution.py
+++ b/solution.py
@@ -154,7 +154,9 @@
             found.append(rows.astype(BF))
         for j in range(CAP):
             hidden = silu(dot_nn(found[j], w_first_ref[feature_width:, :]) + context_part)
-            second = silu(dot_nn(hidden.astype(BF), w_second_ref[...]))
+            found[j] = hidden.astype(BF)
+        for j in range(CAP):
+            second = silu(dot_nn(found[j], w_second_ref[...]))
             score = dot_nt(second.astype(BF), w_score)
             out = jnp.where(lane == core * CAP + j, score, out)
     top = jnp.max(peak, axis=1, keepdims=True)

time: 74.6 us -> 75 us (level)
  no operation moved by 1% of the time
where the time goes in v9:
time: 75 us; the launch traced here: 74.3 us
  starting transfers between devices  26.1 us (35%)
  blocking collectives  22.9 us (31%)
  waiting for transfers between devices  11.8 us (16%)
  Pallas kernels  10.7 us (14%)
  between operations  2.68 us (4%)
    all_to_all x1, starting transfers between devices, body(): lax.all_to_all(message.reshape(chips, ROWS, 128), CHIPS, split_axis=0, co...  23.2 us
    all_to_all x1, blocking collectives, body(): lax.all_to_all(answers.reshape(chips, 1, 128), CHIPS, split_axis=0, conca...  22.9 us
    all_to_all x1, waiting for transfers between devices, body(): lax.all_to_all(message.reshape(chips, ROWS, 128), CHIPS, split_axis=0, co...  11.8 us
    pallas_call x1, Pallas kernels, body(): pl.pallas_call(hold_kernel, out_shape=jax.ShapeDtypeStruct((chips, 128),...  6.06 us
    ppermute x1, starting transfers between devices, body(): other_table = lax.ppermute(item_table, 'core', [(0, 1), (1, 0)])  2.86 us
    pallas_call x1, Pallas kernels, body(): pl.pallas_call(lambda *refs: ask_kernel(plane, chips, item_rows, *refs),...  2.52 us
  transfers between devices with their start and end apart: 2, of which 1 were waited for; matrix products, arithmetic and copies ran while one was open for 0% of the time, Pallas kernels for 2%

profile of v9, /device:TPU:1, one launch (start us, length us, event | category | flops | bytes accessed | tf_op | source)
XLA Modules:
  0.0 74.3 jit_solution(832393995639242602)
XLA Ops:
  0.6 0.0 copy-start
  0.6 2.5 %ask.1 = bf16[2048,128]{1,0:T(8,128)(2,1)} custom-call(bf16[1,256]{1,0:T(2,128)(2,1)} %refs_0_.2, bf16[1,512]{1,0:T(2,128)(2,1)} %refs_1_.2, s32[1,1024]{1,0:T(1,128)} %refs_0_.3), custom_call_target="tpu_custom_call" | custom-call | tf_op jit(solution)/shard_map/ask/pallas_call | solution.py:207
  3.2 23.2 %all-to-all-start = ((bf16[256,8,128]{2,1,0:T(8,128)(2,1)}), bf16[256,8,128]{2,1,0:T(8,128)(2,1)S(1)}, u32[]{:S(2)}, u32[]{:S(2)}) async-start(bf16[256,8,128]{2,1,0:T(8,128)(2,1)} %bitcast.11), calls=%async_computation | async-start | bytes 1048576 | tf_op jit(solution)/shard_map/all_to_all | solution.py:217
  26.4 0.0 copy-done
  26.4 0.0 copy-start.3
  26.4 2.9 %collective-permute-start = (bf16[2048,256]{1,0:T(8,128)(2,1)S(1)}, bf16[2048,256]{1,0:T(8,128)(2,1)}, u32[]{:S(2)}, u32[]{:S(2)}) collective-permute-start(bf16[2048,256]{1,0:T(8,128)(2,1)S(1)} %copy-done), channel_id=1, source_target_pairs={{0,32},{32,0},{1,33},{33,1},{2,34},{34,2},{3,35},{35,3},{4,36},{36... | collective-permute-start | bytes 3145736 | tf_op jit(solution)/shard_map/ppermute | solution.py:216
  30.6 0.0 copy-start.4
  31.2 0.0 copy-done.4
  31.2 0.0 copy-done.3
  31.3 0.0 copy-start.1
  31.3 0.0 copy-start.2
  31.3 1.1 %place.1 = (f32[8,1024]{1,0:T(8,128)S(1)}, bf16[256,1024]{1,0:T(8,128)(2,1)S(1)}) custom-call(s32[1,1024]{1,0:T(1,128)S(1)} %copy-done.3, s32[1]{0:T(128)S(6)} %copy.13.refs_1_, s32[1]{0:T(128)S(6)} %copy.14.refs_2_, s32[1]{0:T(128)S(6)} %copy.15.refs_3_), custom_call_target="tpu_custom_call" | custom-call | flops 20000000000 | bytes 600000 | tf_op jit(solution)/shard_map/place/pallas_call | solution.py:220
  32.4 11.8 %all-to-all-done = bf16[256,8,128]{2,1,0:T(8,128)(2,1)S(1)} async-done(((bf16[256,8,128]{2,1,0:T(8,128)(2,1)}), bf16[256,8,128]{2,1,0:T(8,128)(2,1)S(1)}, u32[]{:S(2)}, u32[]{:S(2)}) %all-to-all-start) | async-done | bytes 524320 | tf_op jit(solution)/shard_map/all_to_all | solution.py:217
  44.2 0.0 collective-permute-done.other_hbm
  44.2 0.0 copy-done.1
  44.2 0.0 copy-done.2
  44.2 6.1 %hold.1 = f32[256,128]{1,0:T(8,128)S(1)} custom-call(bf16[2048,128]{1,0:T(8,128)(2,1)S(1)} %bitcast.8, bf16[2048,256]{1,0:T(8,128)(2,1)S(1)} %copy-done, bf16[2048,256]{1,0:T(8,128)(2,1)} %collective-permute-done.other_hbm, bf16[768,512]{1,0:T(8,128)(2,1)S(1)} %copy-done.1, bf16[512,512]{1,0:T(8,128)(2,1)S(1)} %copy-done.2, ...), custom_call_target="tpu_custom_call" | custom-call | tf_op jit(solution)/shard_map/hold/pallas_call | solution.py:233
  50.3 22.9 %all_to_all.10 = f32[256,1,128]{2,1,0:T(1,128)S(1)} all-to-all(f32[256,1,128]{2,1,0:T(1,128)S(1)} %bitcast.9), channel_id=1, replica_groups=mesh['y'=8,'core'=2,'x'=4,'z'=8] {'z','y','x'}, dimensions={0} | all-to-all | bytes 262144 | tf_op jit(solution)/shard_map/all_to_all | solution.py:246
  73.2 1.0 %own.1 = (f32[1,1024]{1,0:T(1,128)}, f32[1,128]{1,0:T(1,128)}) custom-call(f32[256,128]{1,0:T(8,128)S(1)} %bitcast.10, bf16[256,1024]{1,0:T(8,128)(2,1)S(1)} %get-tuple-element.10.refs_1_, f32[8,1024]{1,0:T(8,128)S(1)} %get-tuple-element.11.refs_2_), custom_call_target="tpu_custom_call" | custom-call | tf_op jit(solution)/shard_map/own/pallas_call | solution.py:250
  (1 shorter events, 0.0 us)
Async XLA Ops:
  0.6 25.7 %copy-start = (bf16[2048,256]{1,0:T(8,128)(2,1)S(1)}, bf16[2048,256]{1,0:T(8,128)(2,1)}, u32[]{:S(2)}) copy-start(bf16[2048,256]{1,0:T(8,128)(2,1)} %own_ref.1) | copy-start | bytes 3145732
  3.2 41.1 %all-to-all-start = ((bf16[256,8,128]{2,1,0:T(8,128)(2,1)}), bf16[256,8,128]{2,1,0:T(8,128)(2,1)S(1)}, u32[]{:S(2)}, u32[]{:S(2)}) async-start(bf16[256,8,128]{2,1,0:T(8,128)(2,1)} %bitcast.11), calls=%async_computation | async-start | bytes 1048576 | tf_op jit(solution)/shard_map/all_to_all | solution.py:217
  26.4 4.9 %copy-start.3 = (s32[1,1024]{1,0:T(1,128)S(1)}, s32[1,1024]{1,0:T(1,128)}, u32[]{:S(2)}) copy-start(s32[1,1024]{1,0:T(1,128)} %refs_0_.3) | copy-start | bytes 12292
  26.4 17.8 %collective-permute-start = (bf16[2048,256]{1,0:T(8,128)(2,1)S(1)}, bf16[2048,256]{1,0:T(8,128)(2,1)}, u32[]{:S(2)}, u32[]{:S(2)}) collective-permute-start(bf16[2048,256]{1,0:T(8,128)(2,1)S(1)} %copy-done), channel_id=1, source_target_pairs={{0,32},{32,0},{1,33},{33,1},{2,34},{34,2},{3,35},{35,3},{4,36},{36... | collective-permute-start | bytes 3145736 | tf_op jit(solution)/shard_map/ppermute | solution.py:216
  30.6 0.7 copy-start.4
  31.3 13.0 %copy-start.1 = (bf16[768,512]{1,0:T(8,128)(2,1)S(1)}, bf16[768,512]{1,0:T(8,128)(2,1)}, u32[]{:S(2)}) copy-start(bf16[768,512]{1,0:T(8,128)(2,1)} %w_first_ref.1) | copy-start | bytes 2359300
  31.3 13.0 %copy-start.2 = (bf16[512,512]{1,0:T(8,128)(2,1)S(1)}, bf16[512,512]{1,0:T(8,128)(2,1)}, u32[]{:S(2)}) copy-start(bf16[512,512]{1,0:T(8,128)(2,1)} %w_second_ref.1) | copy-start | bytes 1572868
